TPU v7x, 32 devices: a whole 2x2x4 slice. The times are simulated.
32 devices in a mesh: rep: 8 (over z, x), tp: 4 (over y, core).
Axes of the slice: x: 2, y: 2, z: 4, core: 2. Of those that a mesh axis runs over, the one named last changes fastest.
Arguments:
- hidden: bfloat16 [8192, 4096], P('rep'), may hold values from -6 to 6
- norm_gain: bfloat16 [4096], replicated, may hold values from 0.099609375 to 1.8984375
- w_query: bfloat16 [4096, 4096], P('rep', 'tp'), may hold values from -0.09375 to 0.09375
- w_keyval: bfloat16 [4096, 1024], P('rep', 'tp'), may hold values from -0.09375 to 0.09375
- w_output: bfloat16 [4096, 4096], P('tp', 'rep'), may hold values from -0.09375 to 0.09375
- cache: bfloat16 [16384, 1024], P('rep'), may hold values from -190 to 190
- lengths: int32 [8, 4], P('rep'), may hold values from 1 to 640, 1024 in all within a row
- prefix: int32 [32], P('rep'), may hold values from 1 to 512, 8192 in all
- out_gain: bfloat16 [4096], replicated, may hold values from 0.099609375 to 1.8984375
Outputs:
- resid: bfloat16 [8192, 4096], P('rep', 'tp')
- normed: bfloat16 [8192, 4096], P('rep', 'tp')
Inputs may be any that keep to these rules, and one draw needn't show every extreme that they name: `lengths`: each row sums to 1024, and some request has 640 new tokens. All prefixes sum to 8192, and some request has a prefix of 512.
All inputs are finite; a program needn't handle non-finite values. No bound on the sum of `prefix` on one device may be relied on, other than what follows from the above.
Results may differ from a plain program's by a relative error of at most 0.0095.
Values may be sent and summed in bfloat16 or wider, within the bound.
No kernel may reach another device: no remote copies, remote signals or barrier semaphores. Data moves between devices by JAX's collectives and lax.ppermute only.
A program may use at most 128 MiB of HBM per device.

v0:
```python
import functools

import jax
import jax.numpy as jnp
import numpy as np
from jax import lax
from jax.experimental import pallas as pl
from jax.experimental.pallas import tpu as pltpu
from jax.sharding import PartitionSpec as P

H = 32
KV = 4
HD = 128
REQ_REP = 4
PREF_MAX = 512

norm_eps = 1e-05
rope_base = 5000000.0
masked_score = -1e30
lowest_peak = -1e25

VMEM_LIMIT = 63 * 1024 * 1024

SMALL = pl.CostEstimate(flops=1024, bytes_accessed=1024, transcendentals=0)


def ring_order(count):
    return list(range(0, count, 2)) + list(range(count - 1, 0, -2))


def bit_reverse(value, bits):
    return sum(((value >> b) & 1) << (bits - 1 - b) for b in range(bits))


def tables(n_rep, n_tp):
    order = ring_order(n_rep)
    place = [order.index(r) for r in range(n_rep)]
    halves = 2 * n_rep // n_tp
    source = np.zeros((n_rep, 2 * n_rep), np.int32)
    piece = np.zeros((n_rep, n_tp, halves), np.int32)
    column = np.zeros((n_rep, n_tp, halves), np.int32)
    last = [0] * halves
    for r in range(n_rep):
        seen = [0] * n_tp
        for k in range(n_rep):
            for h, src in ((0, order[(place[r] - k) % n_rep]), (1, order[(place[r] + k) % n_rep])):
                source[r, 2 * k + h] = src * 2 + h
                dest = src * n_tp // n_rep
                s = seen[dest]
                seen[dest] += 1
                piece[r, dest, s] = 2 * k + h
                column[r, dest, s] = src * 2 + h - dest * halves
                last[s] = max(last[s], k)
    return order, source, piece, column, last


def rope_tables(position):
    half = HD // 2
    freqs = rope_base ** (-(jnp.arange(half, dtype=jnp.float32) * 2.0 / HD))
    angles = position.astype(jnp.float32)[:, None] * freqs[None, :]
    cosine, sine = jnp.cos(angles), jnp.sin(angles)
    return jnp.concatenate([cosine, cosine], 1), jnp.concatenate([-sine, sine], 1)


def request_position(lens, prefs, count):
    token_ids = jnp.arange(count, dtype=jnp.int32)
    ends = jnp.cumsum(lens)
    starts = ends - lens
    segment = jnp.sum((token_ids[:, None] >= ends[None, :]).astype(jnp.int32), axis=1)
    onehot = segment[:, None] == jnp.arange(lens.shape[0], dtype=jnp.int32)[None, :]
    shift = jnp.sum(jnp.where(onehot, (prefs - starts)[None, :], 0), axis=1)
    return token_ids + shift, starts, ends


def skipping(kernel, first, count):
    return lambda *refs: kernel(*refs[:first], *refs[first + count :])


def norm_kernel(h_ref, gain_ref, *rest):
    out_ref = rest[-1]
    values = h_ref[...].astype(jnp.float32)
    meansq = jnp.mean(values * values, axis=-1, keepdims=True)
    gain = gain_ref[...].astype(jnp.float32)
    out_ref[...] = (values * lax.rsqrt(meansq + norm_eps) * gain).astype(jnp.bfloat16)


def input_norm(hidden, gain, also, tile=128):
    rows, model = hidden.shape
    block = pl.BlockSpec((tile, model), lambda i: (i, 0))
    return pl.pallas_call(
        norm_kernel,
        out_shape=jax.ShapeDtypeStruct((rows, model), jnp.bfloat16),
        grid=(rows // tile,),
        in_specs=[block, pl.BlockSpec((1, model), lambda i: (0, 0))]
        + [pl.BlockSpec(memory_space=pl.ANY)] * len(also),
        out_specs=block,
        compiler_params=pltpu.CompilerParams(vmem_limit_bytes=VMEM_LIMIT),
        cost_estimate=SMALL,
        name="input_norm",
    )(hidden, gain.reshape(1, model), *also)


def project_kernel(index, *refs, count, final, has_acc, heads):
    xs, pieces, rest = refs[:count], refs[count : 2 * count], refs[2 * count :]
    x = jnp.concatenate([ref[...] for ref in xs], axis=1)
    weights = jnp.concatenate([ref[...] for ref in pieces], axis=0)
    total = jnp.dot(x, weights, preferred_element_type=jnp.float32)
    if has_acc:
        total = total + rest[0][...]
        rest = rest[1:]
    if not final:
        rest[0][...] = total
        return
    cos_ref, sin_ref, q_ref, k_ref, v_ref = rest
    cosine, sine = cos_ref[...], sin_ref[...]

    def rotate(u):
        return (u * cosine + pltpu.roll(u, HD // 2, 1) * sine).astype(jnp.bfloat16)

    for h in range(heads):
        q_ref[:, h * HD : (h + 1) * HD] = rotate(total[:, h * HD : (h + 1) * HD])
    key = total[:, heads * HD : (heads + 1) * HD]
    k_ref[...] = rotate(key.astype(jnp.bfloat16).astype(jnp.float32))
    v_ref[...] = total[:, (heads + 1) * HD :].astype(jnp.bfloat16)


def project(index, x, pieces, acc=None, rope=None, also=(), tile=256):
    rows, model = x.shape
    depth, width = pieces[0].shape
    count = len(pieces)
    heads = width // HD - 2
    final = rope is not None
    row_block = lambda w: pl.BlockSpec((tile, w), lambda i, *_: (i, 0))
    in_specs = [
        pl.BlockSpec((tile, depth), lambda i, at, k=k: (i, at[k])) for k in range(count)
    ] + [pl.BlockSpec((depth, width), lambda i, *_: (0, 0), pipeline_mode=pl.Buffered(1))] * count
    args = [x] * count + list(pieces)
    if acc is not None:
        in_specs.append(row_block(width))
        args.append(acc)
    if final:
        in_specs += [row_block(HD)] * 2
        args += list(rope)
        out_shape = [
            jax.ShapeDtypeStruct((rows, heads * HD), jnp.bfloat16),
            jax.ShapeDtypeStruct((rows, HD), jnp.bfloat16),
            jax.ShapeDtypeStruct((rows, HD), jnp.bfloat16),
        ]
        out_specs = [row_block(heads * HD), row_block(HD), row_block(HD)]
    else:
        out_shape = jax.ShapeDtypeStruct((rows, width), jnp.float32)
        out_specs = row_block(width)
    kernel = functools.partial(
        project_kernel, count=count, final=final, has_acc=acc is not None, heads=heads
    )
    kernel = skipping(kernel, 1 + len(args), len(also))
    in_specs += [pl.BlockSpec(memory_space=pl.ANY)] * len(also)
    args += list(also)
    return pl.pallas_call(
        kernel,
        out_shape=out_shape,
        grid_spec=pltpu.PrefetchScalarGridSpec(
            num_scalar_prefetch=1, grid=(rows // tile,), in_specs=in_specs, out_specs=out_specs
        ),
        compiler_params=pltpu.CompilerParams(vmem_limit_bytes=VMEM_LIMIT),
        cost_estimate=SMALL,
        name="project",
    )(index, *args)


def attend_kernel(
    scal, q_ref, k_ref, v_ref, c_ref, *rest, first, heads, tq, tk
):
    o_ref, m_ref, acc_ref = rest[-3:]
    base = first + pl.program_id(0) * tq
    rows = heads * tq
    q = jnp.concatenate([q_ref[:, h * HD : (h + 1) * HD] for h in range(heads)], axis=0)
    m_ref[...] = jnp.full((rows, HD), lowest_peak, jnp.float32)
    acc_ref[...] = jnp.zeros((rows, 2 * HD), jnp.float32)
    token = base + lax.broadcasted_iota(jnp.int32, (tq, 1), 0)
    scale = HD ** (-0.5) * 1.4426950408889634

    def update(keys, values, mask):
        width = keys.shape[0]
        s = lax.dot_general(q, keys, (((1,), (1,)), ((), ())), preferred_element_type=jnp.float32)
        s = s.reshape(heads, tq, width) * scale
        s = jnp.where(mask[None], s, masked_score).reshape(rows, width)
        before = m_ref[...]
        peak = jnp.maximum(before, jnp.max(s, axis=1, keepdims=True))
        m_ref[...] = peak
        keep = jnp.exp2(before - peak)
        p = jnp.exp2(s - jnp.concatenate([peak] * (width // HD), axis=1)).astype(jnp.bfloat16)
        wide = jnp.concatenate([values, jnp.ones((width, HD), jnp.bfloat16)], axis=1)
        acc_ref[...] = acc_ref[...] * jnp.concatenate([keep, keep], axis=1) + jnp.dot(
            p, wide, preferred_element_type=jnp.float32
        )

    for r in range(REQ_REP):
        start, end, pref = scal[r], scal[REQ_REP + r], scal[2 * REQ_REP + r]
        inside = (token >= start) & (token < end)

        @pl.when((start < base + tq) & (end > base))
        def _(r=r, start=start, end=end, pref=pref, inside=inside):
            @pl.loop(0, (pref + tk - 1) // tk)
            def _(j):
                at = pl.ds(pl.multiple_of(r * PREF_MAX + j * tk, tk), tk)
                slot = j * tk + lax.broadcasted_iota(jnp.int32, (1, tk), 1)
                update(c_ref[at, :HD], c_ref[at, HD:], inside & (slot < pref))

            @pl.loop(start // tk, (jnp.minimum(end, base + tq) - 1) // tk + 1)
            def _(j):
                at = pl.ds(pl.multiple_of(j * tk, tk), tk)
                other = j * tk + lax.broadcasted_iota(jnp.int32, (1, tk), 1)
                update(k_ref[at, :], v_ref[at, :], inside & (other >= start) & (other <= token))

    out = (acc_ref[:, :HD] / acc_ref[:, HD:]).astype(jnp.bfloat16)
    for h in range(heads):
        o_ref[:, h * HD : (h + 1) * HD] = out[h * tq : (h + 1) * tq]


def attend(scal, q, k, v, cache, first, rows, earlier=None, also=(), tq=128, tk=256):
    heads = q.shape[1] // HD
    tokens, slots = q.shape[0], cache.shape[0]
    whole = lambda r, w: pl.BlockSpec((r, w), lambda i, *_: (0, 0))
    block = pl.BlockSpec((tq, heads * HD), lambda i, *_: (first // tq + i, 0))
    more = ([] if earlier is None else [earlier]) + list(also)
    return pl.pallas_call(
        functools.partial(attend_kernel, first=first, heads=heads, tq=tq, tk=tk),
        out_shape=jax.ShapeDtypeStruct((tokens, heads * HD), jnp.bfloat16),
        grid_spec=pltpu.PrefetchScalarGridSpec(
            num_scalar_prefetch=1,
            grid=(rows // tq,),
            in_specs=[
                block,
                whole(tokens, HD),
                whole(tokens, HD),
                pl.BlockSpec((slots, 2 * HD), lambda i, s: (0, s[3 * REQ_REP])),
            ]
            + [pl.BlockSpec(memory_space=pl.ANY)] * len(more),
            out_specs=block,
            scratch_shapes=[
                pltpu.VMEM((heads * tq, HD), jnp.float32),
                pltpu.VMEM((heads * tq, 2 * HD), jnp.float32),
            ],
        ),
        input_output_aliases={} if earlier is None else {5: 0},
        compiler_params=pltpu.CompilerParams(vmem_limit_bytes=VMEM_LIMIT),
        cost_estimate=SMALL,
        name="attend",
    )(scal, q, k, v, cache, *more)


def output_kernel(choice, a_ref, *rest, count, slots):
    pieces, (keep_ref, send_ref, held, sems) = rest[:count], rest[count:]
    width = keep_ref.shape[2]

    @pl.when(pl.program_id(0) == 0)
    def _():
        for s in range(slots):
            for i in range(count):

                @pl.when(choice[s] == i)
                def _(s=s, i=i):
                    pltpu.make_async_copy(
                        pieces[i], held.at[:, pl.ds(s * width, width)], sems.at[s]
                    ).start()

        for s in range(slots):
            pltpu.make_async_copy(
                pieces[0], held.at[:, pl.ds(s * width, width)], sems.at[s]
            ).wait()

    half = slots // 2
    part = jnp.dot(a_ref[...], held[...], preferred_element_type=jnp.float32)
    part = part.astype(jnp.bfloat16)
    for s in range(half):
        keep_ref[s] = part[:, s * width : (s + 1) * width]
        send_ref[s] = part[:, (half + s) * width : (half + s + 1) * width]


def output_parts(choice, attended, pieces, slots, also=(), tile=512):
    rows, depth = attended.shape
    width = pieces[0].shape[1]
    count = len(pieces)
    half = jax.ShapeDtypeStruct((slots // 2, rows, width), jnp.bfloat16)
    half_block = pl.BlockSpec((slots // 2, tile, width), lambda i, *_: (0, i, 0))
    kernel = functools.partial(output_kernel, count=count, slots=slots)
    return pl.pallas_call(
        skipping(kernel, 2 + count, len(also)),
        out_shape=[half, half],
        grid_spec=pltpu.PrefetchScalarGridSpec(
            num_scalar_prefetch=1,
            grid=(rows // tile,),
            in_specs=[pl.BlockSpec((tile, depth), lambda i, *_: (i, 0))]
            + [pl.BlockSpec(memory_space=pl.ANY)] * (count + len(also)),
            out_specs=[half_block, half_block],
            scratch_shapes=[
                pltpu.VMEM((depth, slots * width), jnp.bfloat16),
                pltpu.SemaphoreType.DMA((slots,)),
            ],
        ),
        compiler_params=pltpu.CompilerParams(vmem_limit_bytes=VMEM_LIMIT),
        cost_estimate=SMALL,
        name="output_parts",
    )(choice, attended, *pieces, *also)


def residual_kernel(where, h_ref, *rest, groups, last):
    keeps, recvs, rest = rest[:groups], rest[groups : 2 * groups], rest[2 * groups :]
    r_ref, ssq_ref = rest[-2:]
    width = keeps[0].shape[2]
    total = rest[1][...] if last else None
    place = 0
    for keep, recv in zip(keeps, recvs):
        for j in range(keep.shape[0]):
            at = slice(None) if last else pl.ds(pl.multiple_of(where[place] * width, width), width)
            place += 1
            proj = keep[j].astype(jnp.float32) + recv[j].astype(jnp.float32)
            resid = (h_ref[:, at].astype(jnp.float32) + proj).astype(jnp.bfloat16)
            r_ref[:, at] = resid
            wide = resid.astype(jnp.float32)
            square = wide * wide
            for i in range(0, width, HD):
                part = square[:, i : i + HD]
                total = part if total is None else total + part
    if last:
        total = lax.dot_general(
            jnp.ones((8, HD), jnp.float32),
            total,
            (((1,), (1,)), ((), ())),
            precision=lax.Precision.HIGHEST,
            preferred_element_type=jnp.float32,
        )
    ssq_ref[...] = total


def residual(where, hidden, keeps, recvs, total_width, earlier=None, tile=512):
    rows = hidden.shape[0]
    groups = len(keeps)
    width = keeps[0].shape[2]
    last = earlier is not None
    parts = [
        pl.BlockSpec((g.shape[0], tile, width), lambda i, *_: (0, i, 0)) for g in keeps + recvs
    ]
    lanes = pl.BlockSpec((tile, HD), lambda i, *_: (i, 0))
    if last:
        in_place = pl.BlockSpec((tile, width), lambda i, w: (i, w[1]))
        out_place = pl.BlockSpec((tile, width), lambda i, w: (i, w[0]))
        more, more_specs = list(earlier), [pl.BlockSpec(memory_space=pl.ANY), lanes]
        aliases = {2 + 2 * groups: 0}
        ssq_shape, ssq_block = (8, rows), pl.BlockSpec((8, tile), lambda i, *_: (0, i))
    else:
        count = where.shape[0] - 1
        in_place = pl.BlockSpec((tile, total_width), lambda i, w: (i, w[count]))
        out_place = pl.BlockSpec((tile, total_width), lambda i, *_: (i, 0))
        more, more_specs, aliases = [], [], {}
        ssq_shape, ssq_block = (rows, HD), lanes
    return pl.pallas_call(
        functools.partial(residual_kernel, groups=groups, last=last),
        out_shape=[
            jax.ShapeDtypeStruct((rows, total_width), jnp.bfloat16),
            jax.ShapeDtypeStruct(ssq_shape, jnp.float32),
        ],
        grid_spec=pltpu.PrefetchScalarGridSpec(
            num_scalar_prefetch=1,
            grid=(rows // tile,),
            in_specs=[in_place] + parts + more_specs,
            out_specs=[out_place, ssq_block],
        ),
        input_output_aliases=aliases,
        compiler_params=pltpu.CompilerParams(vmem_limit_bytes=VMEM_LIMIT),
        cost_estimate=SMALL,
        name="residual",
    )(where, hidden, *keeps, *recvs, *more)


def join_kernel(*refs):
    pass


def join(arrays, *others):
    anywhere = pl.BlockSpec(memory_space=pltpu.HBM)
    count = len(arrays)
    return tuple(
        pl.pallas_call(
            join_kernel,
            out_shape=[jax.ShapeDtypeStruct(p.shape, p.dtype) for p in arrays],
            in_specs=[anywhere] * count + [pl.BlockSpec(memory_space=pl.ANY)] * len(others),
            out_specs=[anywhere] * count,
            input_output_aliases={i: i for i in range(count)},
            compiler_params=pltpu.CompilerParams(vmem_limit_bytes=VMEM_LIMIT),
            cost_estimate=SMALL,
            name="join",
        )(*arrays, *others)
    )


def body(hidden, norm_gain, w_query, w_keyval, w_output, cache, lengths, prefix, out_gain):
    n_rep, n_tp = lax.axis_size("rep"), lax.axis_size("tp")
    rep, tp = lax.axis_index("rep"), lax.axis_index("tp")
    rows, model = hidden.shape
    heads_here = w_query.shape[1] // HD
    order, source, piece, column, last = tables(n_rep, n_tp)
    ahead = [(order[i], order[(i + 1) % n_rep]) for i in range(n_rep)]
    back = [(b, a) for a, b in ahead]
    swap = lambda value, d: lax.ppermute(value, "tp", [(i, i ^ d) for i in range(n_tp)])
    step = lambda pair: (lax.ppermute(pair[0], "rep", ahead), lax.ppermute(pair[1], "rep", back))

    mid = w_output.shape[1] // 2
    out_pairs = [(w_output[:, :mid], w_output[:, mid:])]
    out_pairs.append(step(out_pairs[0]))

    kv_head_of = lambda t: t * heads_here // (H // KV)
    feats = w_keyval.shape[1] // KV
    col = jnp.arange(w_keyval.shape[1], dtype=jnp.int32)[:, None]
    feat = jnp.arange(feats, dtype=jnp.int32)[None, :]
    parts = []
    for d in range(n_tp):
        pick = (col == feat * KV + kv_head_of(tp ^ d)).astype(jnp.bfloat16)
        mine = jnp.dot(w_keyval, pick, preferred_element_type=jnp.float32).astype(jnp.bfloat16)
        parts.append(swap(mine, d) if d else mine)
    mixed = jnp.concatenate(parts, axis=1)
    slot = jnp.arange(mixed.shape[1], dtype=jnp.int32)
    home = ((slot // feats) ^ tp) * feats + slot % feats
    place = (home[:, None] == slot[None, :]).astype(jnp.bfloat16)
    keyval = jnp.dot(mixed, place, preferred_element_type=jnp.float32).astype(jnp.bfloat16)

    joined = jnp.concatenate([w_query, keyval], axis=1)
    depth = joined.shape[0] // 2

    lens = lengths.reshape(-1)
    position, starts, ends = request_position(lens, prefix, rows)
    rope = rope_tables(position)
    scal = jnp.concatenate(
        [starts, ends, prefix, kv_head_of(tp).astype(jnp.int32)[None]]
    ).astype(jnp.int32)

    bits = n_tp.bit_length() - 1
    dests = tp ^ jnp.asarray([bit_reverse(s, bits) for s in range(n_tp)], jnp.int32)
    choice_all = jnp.asarray(piece)[rep][dests]
    column_all = jnp.asarray(column)[rep][tp]
    halves = piece.shape[2]
    choices = [choice_all[:, s] for s in range(halves)]
    where_early = jnp.concatenate([column_all[:-1], tp[None]]).astype(jnp.int32)
    where_last = jnp.stack([column_all[-1], tp * halves + column_all[-1]]).astype(jnp.int32)
    width = model // n_tp
    gain = lax.dynamic_slice_in_dim(out_gain, tp * width, width, 0).astype(jnp.float32)

    first_cut, second_cut = n_rep // 2, n_rep - 2
    index = jnp.asarray(source)[rep]
    cuts = [0, first_cut, second_cut, n_rep]
    indices = [index[2 * low : 2 * high] for low, high in zip(cuts[:-1], cuts[1:])]
    in_pairs = [join((joined[:depth], joined[depth:]), *out_pairs[1])]
    x = input_norm(hidden, norm_gain, in_pairs[0][:1])
    acc, done = None, 0

    def project_arrived(acc, done, rope=None, also=()):
        ready = [p for pair in in_pairs[done:] for p in pair]
        return project(indices[cuts.index(done)], x, ready, acc, rope, also)

    for k in range(1, n_rep):
        arrived = step(in_pairs[-1])
        if k == 2:
            arrived = join(arrived, x)
        if k == 3:
            arrived = join(
                arrived, scal, *rope, *choices, where_early, where_last, gain, *indices
            )
        if k in (first_cut, second_cut):
            acc, done = project_arrived(acc, done), k
            arrived = join(arrived, acc)
        in_pairs.append(arrived)

    out_pairs[1] = join(out_pairs[1], *in_pairs[-1])
    q, k, v = project_arrived(acc, done, rope, out_pairs[1][:1])

    keeps, recvs = [], []

    def stage(s, attended, also=()):
        pieces = [p for pair in out_pairs[: last[s] + 1] for p in pair]
        return output_parts(choices[s], attended, pieces, n_tp, also)

    def exchange(keep, send):
        size, d = keep.shape[0], 1
        while d < n_tp // 2:
            received = swap(send, d)
            size, d = size // 2, d * 2
            total = [
                (keep[i : i + 1].astype(jnp.float32) + received[i : i + 1].astype(jnp.float32)).astype(
                    jnp.bfloat16
                )
                for i in range(2 * size)
            ]
            if d < n_tp // 2:
                keep = jnp.concatenate(total[:size], 0)
                send = jnp.concatenate(total[size:], 0)
        keeps.extend(total[:size])
        return total[size:]

    def collect(raw):
        sends = exchange(*raw)
        recvs.extend(swap(part, n_tp // 2) for part in sends)
        return sends

    shares = [0, 3, 6, 8]
    tq = rows // shares[-1]
    attended, raw, pending = None, None, list(range(halves))
    for flight in range(2, n_rep):
        arrived = step(out_pairs[-1])
        own = list(out_pairs[-1][:1])
        waits = []
        if flight == 2:
            waits = [q]
        elif flight - 3 < len(shares) - 1:
            low, high = shares[flight - 3 : flight - 1]
            attended = attend(
                scal, q, k, v, cache, low * tq, (high - low) * tq, attended, own, tq=tq
            )
            waits = [attended]
        if flight > len(shares):
            gates, sent = list(own), []
            if raw is not None:
                gates, raw = gates + collect(raw), None
                sent = recvs[-1:]
            if last[pending[0]] < flight and len(pending) > 1:
                raw = stage(pending.pop(0), attended, gates)
                *arrived, passed = join((*arrived, raw[1]), *sent)
                raw, waits = (raw[0], passed), []
        out_pairs.append(join(arrived, *waits) if waits else tuple(arrived))

    while pending:
        gates = collect(raw) if raw is not None else []
        raw = stage(pending.pop(0), attended, gates)
    early = residual(where_early, hidden, keeps, recvs, width)
    older = recvs[-1:]
    keeps.clear()
    recvs.clear()
    keep, send = raw
    (send,) = join((send,), *older)
    collect((keep, send))
    resid, ssq = residual(where_last, hidden, keeps, recvs, width, early)

    d = 1
    while d < n_tp:
        ssq = ssq + swap(ssq, d)
        d *= 2
    factor = lax.rsqrt(ssq[0] / model + norm_eps)
    normed = (resid.astype(jnp.float32) * factor[:, None] * gain[None, :]).astype(jnp.bfloat16)
    return (resid, normed)


def solution(mesh):
    placed = (
        P("rep", None),
        P(),
        P("rep", "tp"),
        P("rep", "tp"),
        P("tp", "rep"),
        P("rep", None),
        P("rep", None),
        P("rep"),
        P(),
    )
    return jax.shard_map(
        body,
        mesh=mesh,
        in_specs=placed,
        out_specs=(P("rep", "tp"), P("rep", "tp")),
        check_vma=False,
    )
```

profile of v0, /device:TPU:0, one launch (start us, length us, event | category | flops | bytes accessed | tf_op | source)
XLA Modules:
  0.0 294.9 jit_solution(15636311070662043654)
XLA Ops:
  14.9 6.1 %collective-permute-done.3.refs_2_.refs_0_ = bf16[1024,256]{1,0:T(8,128)(2,1)S(1)} collective-permute-done((bf16[1024,256]{1,0:T(8,128)(2,1)S(1)}, bf16[1024,256]{1,0:T(8,128)(2,1)S(1)}, u32[]{:S(2)}, u32[]{:S(2)}) %collective-permute-start.3) | collective-permute-done | bytes 524320 | tf_op jit(solution)/shard_map/ppermute | solution.py:407
  27.4 11.4 %collective-permute-done.5.refs_11_ = bf16[256,1280]{1,0:T(8,128)(2,1)} collective-permute-done((bf16[256,1280]{1,0:T(8,128)(2,1)}, bf16[256,1280]{1,0:T(8,128)(2,1)}, u32[]{:S(2)}, u32[]{:S(2)}) %collective-permute-start.5) | collective-permute-done | bytes 655392 | tf_op jit(solution)/shard_map/ppermute | solution.py:407
  42.8 3.2 %fusion.12 = (f32[1024,64]{1,0:T(8,128)}, f32[1024,64]{1,0:T(8,128)}, f32[1024,64]{1,0:T(8,128)}) fusion(f32[64]{0:T(128)S(1)} %negate_power_fusion, f32[1024]{0:T(1024)S(1)} %add_convert_fusion.8), kind=kLoop, calls=%fused_computation.35 | loop fusion | flops 131072 | bytes 790784 | tf_op jit(solution)/shard_map/neg | solution.py:62
  46.1 10.7 %input_norm.1.refs_2_.refs_1_.refs_3_.refs_4_.refs_5_.refs_6_.refs_7_.refs_8_ = bf16[1024,4096]{1,0:T(8,128)(2,1)} custom-call(bf16[1024,4096]{1,0:T(8,128)(2,1)} %h_ref.5, bf16[1,4096]{1,0:T(2,128)(2,1)} %reshape.112.gain_ref, bf16[256,1280]{1,0:T(8,128)(2,1)} %get-tuple-element.44.rest_0_.refs_9_), custom_call_target="tpu_custom_call" | custom-call | flops 1024 | bytes 1024 | tf_op jit(solution)/shard_map/input_norm/pallas_call | solution.py:90
  64.5 7.7 %collective-permute-done.10.refs_1_ = bf16[256,1280]{1,0:T(8,128)(2,1)S(1)} collective-permute-done((bf16[256,1280]{1,0:T(8,128)(2,1)}, bf16[256,1280]{1,0:T(8,128)(2,1)S(1)}, u32[]{:S(2)}, u32[]{:S(2)}) %collective-permute-start.10) | collective-permute-done | bytes 655392 | tf_op jit(solution)/shard_map/ppermute | solution.py:407
  75.9 11.3 %project.3.refs_2_.refs_9_ = f32[1024,1280]{1,0:T(8,128)} custom-call(s32[8]{0:T(128)} %slice_bitcast_fusion.1.refs_12_.refs_0_, bf16[1024,4096]{1,0:T(8,128)(2,1)} %input_norm.1.refs_2_.refs_1_.refs_3_.refs_4_.refs_5_.refs_6_.refs_7_.refs_8_, bf16[1024,4096]{1,0:T(8,128)(2,1)} %input_norm.1.refs_2_.refs_1_.refs_3_.refs_4_.refs_5_.refs_6_.refs_7_.refs_8_, ...), custom_call_target="tpu_custom_call" | custom-call | flops 1024 | bytes 1024 | tf_op jit(solution)/shard_map/project/pallas_call | solution.py:159
  90.7 12.9 %collective-permute-done.13.refs_7_ = bf16[256,1280]{1,0:T(8,128)(2,1)} collective-permute-done((bf16[256,1280]{1,0:T(8,128)(2,1)}, bf16[256,1280]{1,0:T(8,128)(2,1)}, u32[]{:S(2)}, u32[]{:S(2)}) %collective-permute-start.13) | collective-permute-done | bytes 655392 | tf_op jit(solution)/shard_map/ppermute | solution.py:407
  105.6 9.4 %project.4.refs_2_.refs_9_ = f32[1024,1280]{1,0:T(8,128)} custom-call(s32[4]{0:T(128)} %get-tuple-element.107.refs_13_.refs_0_, bf16[1024,4096]{1,0:T(8,128)(2,1)} %input_norm.1.refs_2_.refs_1_.refs_3_.refs_4_.refs_5_.refs_6_.refs_7_.refs_8_, bf16[1024,4096]{1,0:T(8,128)(2,1)} %input_norm.1.refs_2_.refs_1_.refs_3_.refs_4_.refs_5_.refs_6_.refs_7_.refs_8_, ...), custom_call_target="tpu_custom_call" | custom-call | flops 1024 | bytes 1024 | tf_op jit(solution)/shard_map/project/pallas_call | solution.py:159
  120.5 12.0 %collective-permute-done.17.refs_2_.refs_7_ = bf16[256,1280]{1,0:T(8,128)(2,1)S(1)} collective-permute-done((bf16[256,1280]{1,0:T(8,128)(2,1)}, bf16[256,1280]{1,0:T(8,128)(2,1)S(1)}, u32[]{:S(2)}, u32[]{:S(2)}) %collective-permute-start.17) | collective-permute-done | bytes 655392 | tf_op jit(solution)/shard_map/ppermute | solution.py:407
  135.4 8.9 %project.5 = (bf16[1024,1024]{1,0:T(8,128)(2,1)}, bf16[1024,128]{1,0:T(8,128)(2,1)}, bf16[1024,128]{1,0:T(8,128)(2,1)}) custom-call(s32[4]{0:T(128)} %get-tuple-element.108.refs_14_.refs_0_, bf16[1024,4096]{1,0:T(8,128)(2,1)} %input_norm.1.refs_2_.refs_1_.refs_3_.refs_4_.refs_5_.refs_6_.refs_7_.refs_8_, ...), custom_call_target="tpu_custom_call" | custom-call | flops 1024 | bytes 1024 | tf_op jit(solution)/shard_map/project/pallas_call | solution.py:159
  150.2 11.4 %attend.3.refs_2_.rest_0_ = bf16[1024,1024]{1,0:T(8,128)(2,1)} custom-call(s32[13]{0:T(128)} %pad_add_fusion.1.refs_2_.scal, bf16[1024,1024]{1,0:T(8,128)(2,1)} %get-tuple-element.55.refs_2_.q_ref, bf16[1024,128]{1,0:T(8,128)(2,1)} %get-tuple-element.56.k_ref, bf16[1024,128]{1,0:T(8,128)(2,1)} %get-tuple-element.57.v_ref, bf16[2048,1024]{1,0:T(8,128)(2,1)} %c_ref.5, ...), custom_call_target="tpu_custom_call" | custom-call | flops 1024 | bytes 1024 | tf_op jit(solution)/shard_map/attend/pallas_call | solution.py:227
  165.9 14.6 %attend.4.refs_2_.rest_0_ = bf16[1024,1024]{1,0:T(8,128)(2,1)} custom-call(s32[13]{0:T(128)} %pad_add_fusion.1.refs_2_.scal, bf16[1024,1024]{1,0:T(8,128)(2,1)} %get-tuple-element.55.refs_2_.q_ref, bf16[1024,128]{1,0:T(8,128)(2,1)} %get-tuple-element.56.k_ref, bf16[1024,128]{1,0:T(8,128)(2,1)} %get-tuple-element.57.v_ref, ...), custom_call_target="tpu_custom_call", output_to_operand_aliasing={{}: (5, {})} | custom-call | flops 1024 | bytes 1024 | tf_op jit(solution)/shard_map/attend/pallas_call | solution.py:227
  183.4 9.8 %attend.5.refs_1_ = bf16[1024,1024]{1,0:T(8,128)(2,1)} custom-call(s32[13]{0:T(128)} %pad_add_fusion.1.refs_2_.scal, bf16[1024,1024]{1,0:T(8,128)(2,1)} %get-tuple-element.55.refs_2_.q_ref, bf16[1024,128]{1,0:T(8,128)(2,1)} %get-tuple-element.56.k_ref, bf16[1024,128]{1,0:T(8,128)(2,1)} %get-tuple-element.57.v_ref, ...), custom_call_target="tpu_custom_call", output_to_operand_aliasing={{}: (5, {})} | custom-call | flops 1024 | bytes 1024 | tf_op jit(solution)/shard_map/attend/pallas_call | solution.py:227
  193.2 7.0 %output_parts.4 = (bf16[2,1024,256]{2,1,0:T(8,128)(2,1)}, bf16[2,1024,256]{2,1,0:T(8,128)(2,1)}) custom-call(s32[4]{0:T(128)} %get-tuple-element.88.refs_5_.refs_0_, bf16[1024,1024]{1,0:T(8,128)(2,1)} %attend.5.refs_1_, bf16[1024,256]{1,0:T(8,128)(2,1)} %copy-done.7, bf16[1024,256]{1,0:T(8,128)(2,1)} %copy-done.6, ...), custom_call_target="tpu_custom_call" | custom-call | flops 1024 | bytes 1024 | tf_op jit(solution)/shard_map/output_parts/pallas_call | solution.py:288
  208.0 7.0 %output_parts.5 = (bf16[2,1024,256]{2,1,0:T(8,128)(2,1)}, bf16[2,1024,256]{2,1,0:T(8,128)(2,1)}) custom-call(s32[4]{0:T(128)} %get-tuple-element.87.refs_6_.refs_0_, bf16[1024,1024]{1,0:T(8,128)(2,1)} %attend.5.refs_1_, bf16[1024,256]{1,0:T(8,128)(2,1)} %copy-done.7, bf16[1024,256]{1,0:T(8,128)(2,1)} %copy-done.6, ...), custom_call_target="tpu_custom_call" | custom-call | flops 1024 | bytes 1024 | tf_op jit(solution)/shard_map/output_parts/pallas_call | solution.py:288
  216.1 4.6 %collective-permute-done.30.refs_3_.rest_3_ = bf16[1,1024,256]{2,1,0:T(8,128)(2,1)} collective-permute-done((bf16[1,1024,256]{2,1,0:T(8,128)(2,1)}, bf16[1,1024,256]{2,1,0:T(8,128)(2,1)}, u32[]{:S(2)}, u32[]{:S(2)}) %collective-permute-start.30) | collective-permute-done | bytes 524320 | tf_op jit(solution)/shard_map/ppermute | solution.py:406
  227.6 7.0 %output_parts.6 = (bf16[2,1024,256]{2,1,0:T(8,128)(2,1)}, bf16[2,1024,256]{2,1,0:T(8,128)(2,1)}) custom-call(s32[4]{0:T(128)} %get-tuple-element.86.refs_7_.refs_0_, bf16[1024,1024]{1,0:T(8,128)(2,1)} %attend.5.refs_1_, bf16[1024,256]{1,0:T(8,128)(2,1)} %copy-done.7, bf16[1024,256]{1,0:T(8,128)(2,1)} %copy-done.6, ...), custom_call_target="tpu_custom_call" | custom-call | flops 1024 | bytes 1024 | tf_op jit(solution)/shard_map/output_parts/pallas_call | solution.py:288
  235.8 4.5 %collective-permute-done.34.refs_3_.rest_4_ = bf16[1,1024,256]{2,1,0:T(8,128)(2,1)S(1)} collective-permute-done((bf16[1,1024,256]{2,1,0:T(8,128)(2,1)}, bf16[1,1024,256]{2,1,0:T(8,128)(2,1)S(1)}, u32[]{:S(2)}, u32[]{:S(2)}) %collective-permute-start.34) | collective-permute-done | bytes 524320 | tf_op jit(solution)/shard_map/ppermute | solution.py:406
  247.9 7.0 %output_parts.7 = (bf16[2,1024,256]{2,1,0:T(8,128)(2,1)}, bf16[2,1024,256]{2,1,0:T(8,128)(2,1)}) custom-call(s32[4]{0:T(128)} %get-tuple-element.89.refs_8_.refs_0_, bf16[1024,1024]{1,0:T(8,128)(2,1)} %attend.5.refs_1_, bf16[1024,256]{1,0:T(8,128)(2,1)} %copy-done.7, bf16[1024,256]{1,0:T(8,128)(2,1)} %copy-done.6, ...), custom_call_target="tpu_custom_call" | custom-call | flops 1024 | bytes 1024 | tf_op jit(solution)/shard_map/output_parts/pallas_call | solution.py:288
  255.0 5.6 %collective-permute-done.36.refs_1_.rest_5_ = bf16[1,1024,256]{2,1,0:T(8,128)(2,1)S(1)} collective-permute-done((bf16[1,1024,256]{2,1,0:T(8,128)(2,1)}, bf16[1,1024,256]{2,1,0:T(8,128)(2,1)S(1)}, u32[]{:S(2)}, u32[]{:S(2)}) %collective-permute-start.36) | collective-permute-done | bytes 524320 | tf_op jit(solution)/shard_map/ppermute | solution.py:406
  268.3 5.0 %residual.2 = (bf16[1024,1024]{1,0:T(8,128)(2,1)}, f32[1024,128]{1,0:T(8,128)}) custom-call(s32[4]{0:T(128)} %pad_add_fusion.2.refs_9_.where, bf16[1024,4096]{1,0:T(8,128)(2,1)} %h_ref.5, bf16[1,1024,256]{2,1,0:T(8,128)(2,1)} %get-tuple-element.96.rest_0_, bf16[1,1024,256]{2,1,0:T(8,128)(2,1)} %get-tuple-element.94.rest_1_, ...), custom_call_target="tpu_custom_call" | custom-call | flops 1024 | bytes 1024 | tf_op jit(solution)/shard_map/residual/pallas_call | solution.py:358
  273.2 7.7 %collective-permute-done.38.rest_1_ = bf16[1,1024,256]{2,1,0:T(8,128)(2,1)S(1)} collective-permute-done((bf16[1,1024,256]{2,1,0:T(8,128)(2,1)}, bf16[1,1024,256]{2,1,0:T(8,128)(2,1)S(1)}, u32[]{:S(2)}, u32[]{:S(2)}) %collective-permute-start.38) | collective-permute-done | bytes 524320 | tf_op jit(solution)/shard_map/ppermute | solution.py:406
  281.7 3.5 %residual.3 = (bf16[1024,1024]{1,0:T(8,128)(2,1)}, f32[8,1024]{1,0:T(8,128)}) custom-call(s32[2]{0:T(128)} %pad_add_fusion.refs_10_.where, bf16[1024,4096]{1,0:T(8,128)(2,1)} %h_ref.5, bf16[1,1024,256]{2,1,0:T(8,128)(2,1)} %get-tuple-element.99.rest_0_, bf16[1,1024,256]{2,1,0:T(8,128)(2,1)} %copy-done.18, ...), custom_call_target="tpu_custom_call", output_to_operand_aliasing={{0}: (4, {})} | custom-call | flops 1024 | bytes 1024 | tf_op jit(solution)/shard_map/residual/pallas_call | solution.py:358
  291.4 3.5 %multiply_convert_fusion = bf16[1024,1024]{1,0:T(8,128)(2,1)} fusion(bf16[1024,1024]{1,0:T(8,128)(2,1)} %get-tuple-element.42, f32[1024]{0:T(1024)S(1)} %copy-done.19, f32[1024]{0:T(1024)S(1)} %bitcast.35), kind=kLoop, calls=%fused_computation.1 | loop fusion | flops 4194304 | bytes 4202496 | tf_op jit(solution)/shard_map/convert_element_type | solution.py:548
  (175 shorter events, 101.2 us)
Async XLA Ops:
  6.9 14.1 %collective-permute-start.3 = (bf16[1024,256]{1,0:T(8,128)(2,1)S(1)}, bf16[1024,256]{1,0:T(8,128)(2,1)S(1)}, u32[]{:S(2)}, u32[]{:S(2)}) collective-permute-start(bf16[1024,256]{1,0:T(8,128)(2,1)S(1)} %get-tuple-element.103.refs_2_), channel_id=1, source_target_pairs={{0,8},{8,16},{16,24},{24,28},{28,20},{20,12},{12,4},{4,0},{1,9},{9... | collective-permute-start | bytes 1572872 | tf_op jit(solution)/shard_map/ppermute | solution.py:407
  8.7 14.0 %collective-permute-start.4 = (bf16[1024,256]{1,0:T(8,128)(2,1)S(1)}, bf16[1024,256]{1,0:T(8,128)(2,1)}, u32[]{:S(2)}, u32[]{:S(2)}) collective-permute-start(bf16[1024,256]{1,0:T(8,128)(2,1)S(1)} %get-tuple-element.102.refs_3_), channel_id=1, source_target_pairs={{8,0},{16,8},{24,16},{28,24},{20,28},{12,20},{4,12},{0,4},{9,1},{1... | collective-permute-start | bytes 1572872 | tf_op jit(solution)/shard_map/ppermute | solution.py:407
  22.6 16.2 %collective-permute-start.5 = (bf16[256,1280]{1,0:T(8,128)(2,1)}, bf16[256,1280]{1,0:T(8,128)(2,1)}, u32[]{:S(2)}, u32[]{:S(2)}) collective-permute-start(bf16[256,1280]{1,0:T(8,128)(2,1)} %get-tuple-element.44.rest_0_.refs_9_), channel_id=1, source_target_pairs={{0,8},{8,16},{16,24},{24,28},{28,20},{20,12},{12,4},{4,0},{1,9},{9... | collective-permute-start | bytes 1966088 | tf_op jit(solution)/shard_map/ppermute | solution.py:407
  24.2 16.2 %collective-permute-start.7 = (bf16[256,1280]{1,0:T(8,128)(2,1)}, bf16[256,1280]{1,0:T(8,128)(2,1)}, u32[]{:S(2)}, u32[]{:S(2)}) collective-permute-start(bf16[256,1280]{1,0:T(8,128)(2,1)} %get-tuple-element.45.refs_10_), channel_id=1, source_target_pairs={{8,0},{16,8},{24,16},{28,24},{20,28},{12,20},{4,12},{0,4},{9,1},{1... | collective-permute-start | bytes 1966088 | tf_op jit(solution)/shard_map/ppermute | solution.py:407
  38.8 18.0 %collective-permute-start.6 = (bf16[256,1280]{1,0:T(8,128)(2,1)}, bf16[256,1280]{1,0:T(8,128)(2,1)S(1)}, u32[]{:S(2)}, u32[]{:S(2)}) collective-permute-start(bf16[256,1280]{1,0:T(8,128)(2,1)} %collective-permute-done.5.refs_11_), channel_id=1, source_target_pairs={{0,8},{8,16},{16,24},{24,28},{28,20},{20,12},{12,4},{4,0},{1,9},{9... | collective-permute-start | bytes 1966088 | tf_op jit(solution)/shard_map/ppermute | solution.py:407
  40.4 16.4 %collective-permute-start.8 = (bf16[256,1280]{1,0:T(8,128)(2,1)}, bf16[256,1280]{1,0:T(8,128)(2,1)}, u32[]{:S(2)}, u32[]{:S(2)}) collective-permute-start(bf16[256,1280]{1,0:T(8,128)(2,1)} %collective-permute-done.7.refs_12_), channel_id=1, source_target_pairs={{8,0},{16,8},{24,16},{28,24},{20,28},{12,20},{4,12},{0,4},{9,1},{1... | collective-permute-start | bytes 1966088 | tf_op jit(solution)/shard_map/ppermute | solution.py:407
  57.7 14.6 %collective-permute-start.10 = (bf16[256,1280]{1,0:T(8,128)(2,1)}, bf16[256,1280]{1,0:T(8,128)(2,1)S(1)}, u32[]{:S(2)}, u32[]{:S(2)}) collective-permute-start(bf16[256,1280]{1,0:T(8,128)(2,1)} %get-tuple-element.47.refs_14_), channel_id=1, source_target_pairs={{8,0},{16,8},{24,16},{28,24},{20,28},{12,20},{4,12},{0,4},{9,1},{1... | collective-permute-start | bytes 1966088 | tf_op jit(solution)/shard_map/ppermute | solution.py:407
  59.0 14.9 %collective-permute-start.9 = (bf16[256,1280]{1,0:T(8,128)(2,1)}, bf16[256,1280]{1,0:T(8,128)(2,1)}, u32[]{:S(2)}, u32[]{:S(2)}) collective-permute-start(bf16[256,1280]{1,0:T(8,128)(2,1)} %get-tuple-element.46.refs_13_), channel_id=1, source_target_pairs={{0,8},{8,16},{16,24},{24,28},{28,20},{20,12},{12,4},{4,0},{1,9},{9... | collective-permute-start | bytes 1966088 | tf_op jit(solution)/shard_map/ppermute | solution.py:407
  88.6 14.9 %collective-permute-start.13 = (bf16[256,1280]{1,0:T(8,128)(2,1)}, bf16[256,1280]{1,0:T(8,128)(2,1)}, u32[]{:S(2)}, u32[]{:S(2)}) collective-permute-start(bf16[256,1280]{1,0:T(8,128)(2,1)} %get-tuple-element.50.refs_5_), channel_id=1, source_target_pairs={{0,8},{8,16},{16,24},{24,28},{28,20},{20,12},{12,4},{4,0},{1,9},{9... | collective-permute-start | bytes 1966088 | tf_op jit(solution)/shard_map/ppermute | solution.py:407
  89.9 14.9 %collective-permute-start.15 = (bf16[256,1280]{1,0:T(8,128)(2,1)}, bf16[256,1280]{1,0:T(8,128)(2,1)}, u32[]{:S(2)}, u32[]{:S(2)}) collective-permute-start(bf16[256,1280]{1,0:T(8,128)(2,1)} %get-tuple-element.51.refs_6_), channel_id=1, source_target_pairs={{8,0},{16,8},{24,16},{28,24},{20,28},{12,20},{4,12},{0,4},{9,1},{1... | collective-permute-start | bytes 1966088 | tf_op jit(solution)/shard_map/ppermute | solution.py:407
  118.5 14.0 %collective-permute-start.17 = (bf16[256,1280]{1,0:T(8,128)(2,1)}, bf16[256,1280]{1,0:T(8,128)(2,1)S(1)}, u32[]{:S(2)}, u32[]{:S(2)}) collective-permute-start(bf16[256,1280]{1,0:T(8,128)(2,1)} %get-tuple-element.52.refs_5_), channel_id=1, source_target_pairs={{0,8},{8,16},{16,24},{24,28},{28,20},{20,12},{12,4},{4,0},{1,9},{9... | collective-permute-start | bytes 1966088 | tf_op jit(solution)/shard_map/ppermute | solution.py:407
  149.8 14.1 %collective-permute-start.22 = (bf16[1024,256]{1,0:T(8,128)(2,1)}, bf16[1024,256]{1,0:T(8,128)(2,1)}, u32[]{:S(2)}, u32[]{:S(2)}) collective-permute-start(bf16[1024,256]{1,0:T(8,128)(2,1)} %get-tuple-element.60.refs_7_), channel_id=1, source_target_pairs={{8,0},{16,8},{24,16},{28,24},{20,28},{12,20},{4,12},{0,4},{9,1},{1... | collective-permute-start | bytes 1572872 | tf_op jit(solution)/shard_map/ppermute | solution.py:407
  163.9 16.7 %collective-permute-start.23 = (bf16[1024,256]{1,0:T(8,128)(2,1)}, bf16[1024,256]{1,0:T(8,128)(2,1)S(1)}, u32[]{:S(2)}, u32[]{:S(2)}) collective-permute-start(bf16[1024,256]{1,0:T(8,128)(2,1)} %get-tuple-element.61.rest_1_.refs_8_), channel_id=1, source_target_pairs={{0,8},{8,16},{16,24},{24,28},{28,20},{20,12},{12,4},{4,0},{1,9},{9... | collective-permute-start | bytes 1572872 | tf_op jit(solution)/shard_map/ppermute | solution.py:407
  164.7 15.9 %collective-permute-start.24 = (bf16[1024,256]{1,0:T(8,128)(2,1)}, bf16[1024,256]{1,0:T(8,128)(2,1)}, u32[]{:S(2)}, u32[]{:S(2)}) collective-permute-start(bf16[1024,256]{1,0:T(8,128)(2,1)} %get-tuple-element.62.refs_9_), channel_id=1, source_target_pairs={{8,0},{16,8},{24,16},{28,24},{20,28},{12,20},{4,12},{0,4},{9,1},{1... | collective-permute-start | bytes 1572872 | tf_op jit(solution)/shard_map/ppermute | solution.py:407
  181.4 18.9 %collective-permute-start.25 = (bf16[1024,256]{1,0:T(8,128)(2,1)}, bf16[1024,256]{1,0:T(8,128)(2,1)S(1)}, u32[]{:S(2)}, u32[]{:S(2)}) collective-permute-start(bf16[1024,256]{1,0:T(8,128)(2,1)} %get-tuple-element.63.rest_1_.refs_10_), channel_id=1, source_target_pairs={{0,8},{8,16},{16,24},{24,28},{28,20},{20,12},{12,4},{4,0},{1,9},{9... | collective-permute-start | bytes 1572872 | tf_op jit(solution)/shard_map/ppermute | solution.py:407
  181.4 18.9 %collective-permute-start.26 = (bf16[1024,256]{1,0:T(8,128)(2,1)}, bf16[1024,256]{1,0:T(8,128)(2,1)}, u32[]{:S(2)}, u32[]{:S(2)}) collective-permute-start(bf16[1024,256]{1,0:T(8,128)(2,1)} %get-tuple-element.64.refs_11_), channel_id=1, source_target_pairs={{8,0},{16,8},{24,16},{28,24},{20,28},{12,20},{4,12},{0,4},{9,1},{1... | collective-permute-start | bytes 1572872 | tf_op jit(solution)/shard_map/ppermute | solution.py:407
  201.1 14.5 %collective-permute-start.27 = (bf16[1024,256]{1,0:T(8,128)(2,1)}, bf16[1024,256]{1,0:T(8,128)(2,1)S(1)}, u32[]{:S(2)}, u32[]{:S(2)}) collective-permute-start(bf16[1024,256]{1,0:T(8,128)(2,1)} %get-tuple-element.66.refs_12_), channel_id=1, source_target_pairs={{0,8},{8,16},{16,24},{24,28},{28,20},{20,12},{12,4},{4,0},{1,9},{9... | collective-permute-start | bytes 1572872 | tf_op jit(solution)/shard_map/ppermute | solution.py:407
  201.7 14.4 %collective-permute-start.28 = (bf16[1024,256]{1,0:T(8,128)(2,1)}, bf16[1024,256]{1,0:T(8,128)(2,1)}, u32[]{:S(2)}, u32[]{:S(2)}) collective-permute-start(bf16[1024,256]{1,0:T(8,128)(2,1)} %get-tuple-element.67.refs_13_), channel_id=1, source_target_pairs={{8,0},{16,8},{24,16},{28,24},{20,28},{12,20},{4,12},{0,4},{9,1},{1... | collective-permute-start | bytes 1572872 | tf_op jit(solution)/shard_map/ppermute | solution.py:407
  206.4 14.3 %collective-permute-start.30 = (bf16[1,1024,256]{2,1,0:T(8,128)(2,1)}, bf16[1,1024,256]{2,1,0:T(8,128)(2,1)}, u32[]{:S(2)}, u32[]{:S(2)}) collective-permute-start(bf16[1,1024,256]{2,1,0:T(8,128)(2,1)} %get-tuple-element.97.refs_13_), channel_id=1, source_target_pairs={{0,2},{1,3},{2,0},{3,1},{4,6},{5,7},{6,4},{7,5},{8,10},{9,11},{10,... | collective-permute-start | bytes 1572872 | tf_op jit(solution)/shard_map/ppermute | solution.py:406
  220.7 14.7 %collective-permute-start.31 = (bf16[1024,256]{1,0:T(8,128)(2,1)}, bf16[1024,256]{1,0:T(8,128)(2,1)}, u32[]{:S(2)}, u32[]{:S(2)}) collective-permute-start(bf16[1024,256]{1,0:T(8,128)(2,1)} %get-tuple-element.71.refs_14_.refs_16_), channel_id=1, source_target_pairs={{0,8},{8,16},{16,24},{24,28},{28,20},{20,12},{12,4},{4,0},{1,9},{9... | collective-permute-start | bytes 1572872 | tf_op jit(solution)/shard_map/ppermute | solution.py:407
  221.4 14.4 %collective-permute-start.32 = (bf16[1024,256]{1,0:T(8,128)(2,1)}, bf16[1024,256]{1,0:T(8,128)(2,1)}, u32[]{:S(2)}, u32[]{:S(2)}) collective-permute-start(bf16[1024,256]{1,0:T(8,128)(2,1)} %get-tuple-element.72.refs_15_), channel_id=1, source_target_pairs={{8,0},{16,8},{24,16},{28,24},{20,28},{12,20},{4,12},{0,4},{9,1},{1... | collective-permute-start | bytes 1572872 | tf_op jit(solution)/shard_map/ppermute | solution.py:407
  226.1 14.2 %collective-permute-start.34 = (bf16[1,1024,256]{2,1,0:T(8,128)(2,1)}, bf16[1,1024,256]{2,1,0:T(8,128)(2,1)S(1)}, u32[]{:S(2)}, u32[]{:S(2)}) collective-permute-start(bf16[1,1024,256]{2,1,0:T(8,128)(2,1)} %get-tuple-element.95.refs_17_), channel_id=1, source_target_pairs={{0,2},{1,3},{2,0},{3,1},{4,6},{5,7},{6,4},{7,5},{8,10},{9,11},{10,... | collective-permute-start | bytes 1572872 | tf_op jit(solution)/shard_map/ppermute | solution.py:406
  246.4 14.2 %collective-permute-start.36 = (bf16[1,1024,256]{2,1,0:T(8,128)(2,1)}, bf16[1,1024,256]{2,1,0:T(8,128)(2,1)S(1)}, u32[]{:S(2)}, u32[]{:S(2)}) collective-permute-start(bf16[1,1024,256]{2,1,0:T(8,128)(2,1)} %get-tuple-element.93.refs_18_), channel_id=1, source_target_pairs={{0,2},{1,3},{2,0},{3,1},{4,6},{5,7},{6,4},{7,5},{8,10},{9,11},{10,... | collective-permute-start | bytes 1572872 | tf_op jit(solution)/shard_map/ppermute | solution.py:406
  266.8 14.2 %collective-permute-start.38 = (bf16[1,1024,256]{2,1,0:T(8,128)(2,1)}, bf16[1,1024,256]{2,1,0:T(8,128)(2,1)S(1)}, u32[]{:S(2)}, u32[]{:S(2)}) collective-permute-start(bf16[1,1024,256]{2,1,0:T(8,128)(2,1)} %get-tuple-element.98), channel_id=1, source_target_pairs={{0,2},{1,3},{2,0},{3,1},{4,6},{5,7},{6,4},{7,5},{8,10},{9,11},{10,... | collective-permute-start | bytes 1572872 | tf_op jit(solution)/shard_map/ppermute | solution.py:406
  (41 other events, 269.8 us)
where the time goes:
time: 296 us; the launch traced here: 295 us
  Pallas kernels  113 us (38%)
  waiting for transfers between devices  101 us (34%)
  starting transfers between devices  39.1 us (13%)
  other arithmetic  25.9 us (9%)
  local copies, waits for them, and re-layouts  13.2 us (4%)
    ppermute x14, waiting for transfers between devices, body(): lax.ppermute(pair[0], 'rep', ahead)  50.5 us
    pallas_call x3, Pallas kernels, attend(): pl.pallas_call(functools.partial(attend_kernel, first=first, heads=heads,...  35.9 us
    ppermute x13, waiting for transfers between devices, body(): lax.ppermute(value, 'tp', [(i, i ^ d) for i in range(n_tp)])  33.7 us
    pallas_call x3, Pallas kernels, project(): pl.pallas_call(kernel, out_shape=out_shape, grid_spec=pltpu.PrefetchScala...  29.6 us
    pallas_call x4, Pallas kernels, output_parts(): pl.pallas_call(skipping(kernel, 2 + count, len(also)), out_shape=[half, h...  28.2 us
    ppermute x14, waiting for transfers between devices, body(): lax.ppermute(pair[1], 'rep', back)  16.9 us
    ppermute x14, starting transfers between devices, body(): lax.ppermute(pair[0], 'rep', ahead)  15.9 us
    ppermute x14, starting transfers between devices, body(): lax.ppermute(pair[1], 'rep', back)  12.3 us
  transfers between devices with their start and end apart: 41, of which 31 were waited for; matrix products, arithmetic and copies ran while one was open for 8% of the time, Pallas kernels for 37%

commit v1 on v0

--- a/solution.py
+++ b/solution.py
@@ -251,8 +251,8 @@
 
 
 def output_kernel(choice, a_ref, *rest, count, slots):
-    pieces, (keep_ref, send_ref, held, sems) = rest[:count], rest[count:]
-    width = keep_ref.shape[2]
+    pieces, outs, (held, sems) = rest[:count], rest[count : count + slots], rest[count + slots :]
+    width = outs[0].shape[1]
 
     @pl.when(pl.program_id(0) == 0)
     def _():
@@ -270,30 +270,26 @@
                 pieces[0], held.at[:, pl.ds(s * width, width)], sems.at[s]
             ).wait()
 
-    half = slots // 2
     part = jnp.dot(a_ref[...], held[...], preferred_element_type=jnp.float32)
     part = part.astype(jnp.bfloat16)
-    for s in range(half):
-        keep_ref[s] = part[:, s * width : (s + 1) * width]
-        send_ref[s] = part[:, (half + s) * width : (half + s + 1) * width]
+    for s in range(slots):
+        outs[s][...] = part[:, s * width : (s + 1) * width]
 
 
 def output_parts(choice, attended, pieces, slots, also=(), tile=512):
     rows, depth = attended.shape
     width = pieces[0].shape[1]
     count = len(pieces)
-    half = jax.ShapeDtypeStruct((slots // 2, rows, width), jnp.bfloat16)
-    half_block = pl.BlockSpec((slots // 2, tile, width), lambda i, *_: (0, i, 0))
     kernel = functools.partial(output_kernel, count=count, slots=slots)
     return pl.pallas_call(
         skipping(kernel, 2 + count, len(also)),
-        out_shape=[half, half],
+        out_shape=[jax.ShapeDtypeStruct((rows, width), jnp.bfloat16)] * slots,
         grid_spec=pltpu.PrefetchScalarGridSpec(
             num_scalar_prefetch=1,
             grid=(rows // tile,),
             in_specs=[pl.BlockSpec((tile, depth), lambda i, *_: (i, 0))]
             + [pl.BlockSpec(memory_space=pl.ANY)] * (count + len(also)),
-            out_specs=[half_block, half_block],
+            out_specs=[pl.BlockSpec((tile, width), lambda i, *_: (i, 0))] * slots,
             scratch_shapes=[
                 pltpu.VMEM((depth, slots * width), jnp.bfloat16),
                 pltpu.SemaphoreType.DMA((slots,)),
@@ -305,24 +301,21 @@
     )(choice, attended, *pieces, *also)
 
 
-def residual_kernel(where, h_ref, *rest, groups, last):
-    keeps, recvs, rest = rest[:groups], rest[groups : 2 * groups], rest[2 * groups :]
+def residual_kernel(where, h_ref, *rest, stages, last):
+    terms, rest = rest[: 3 * stages], rest[3 * stages :]
     r_ref, ssq_ref = rest[-2:]
-    width = keeps[0].shape[2]
+    width = terms[0].shape[1]
     total = rest[1][...] if last else None
-    place = 0
-    for keep, recv in zip(keeps, recvs):
-        for j in range(keep.shape[0]):
-            at = slice(None) if last else pl.ds(pl.multiple_of(where[place] * width, width), width)
-            place += 1
-            proj = keep[j].astype(jnp.float32) + recv[j].astype(jnp.float32)
-            resid = (h_ref[:, at].astype(jnp.float32) + proj).astype(jnp.bfloat16)
-            r_ref[:, at] = resid
-            wide = resid.astype(jnp.float32)
-            square = wide * wide
-            for i in range(0, width, HD):
-                part = square[:, i : i + HD]
-                total = part if total is None else total + part
+    for s in range(stages):
+        at = slice(None) if last else pl.ds(pl.multiple_of(where[s] * width, width), width)
+        proj = sum(term[...].astype(jnp.float32) for term in terms[3 * s : 3 * s + 3])
+        resid = (h_ref[:, at].astype(jnp.float32) + proj).astype(jnp.bfloat16)
+        r_ref[:, at] = resid
+        wide = resid.astype(jnp.float32)
+        square = wide * wide
+        for i in range(0, width, HD):
+            part = square[:, i : i + HD]
+            total = part if total is None else total + part
     if last:
         total = lax.dot_general(
             jnp.ones((8, HD), jnp.float32),
@@ -334,20 +327,19 @@
     ssq_ref[...] = total
 
 
-def residual(where, hidden, keeps, recvs, total_width, earlier=None, tile=512):
+def residual(where, hidden, terms, total_width, earlier=None, tile=512):
     rows = hidden.shape[0]
-    groups = len(keeps)
-    width = keeps[0].shape[2]
+    stages = len(terms)
+    terms = [term for stage in terms for term in stage]
+    width = terms[0].shape[1]
     last = earlier is not None
-    parts = [
-        pl.BlockSpec((g.shape[0], tile, width), lambda i, *_: (0, i, 0)) for g in keeps + recvs
-    ]
+    parts = [pl.BlockSpec((tile, width), lambda i, *_: (i, 0))] * len(terms)
     lanes = pl.BlockSpec((tile, HD), lambda i, *_: (i, 0))
     if last:
         in_place = pl.BlockSpec((tile, width), lambda i, w: (i, w[1]))
         out_place = pl.BlockSpec((tile, width), lambda i, w: (i, w[0]))
         more, more_specs = list(earlier), [pl.BlockSpec(memory_space=pl.ANY), lanes]
-        aliases = {2 + 2 * groups: 0}
+        aliases = {2 + len(terms): 0}
         ssq_shape, ssq_block = (8, rows), pl.BlockSpec((8, tile), lambda i, *_: (0, i))
     else:
         count = where.shape[0] - 1
@@ -356,7 +348,7 @@
         more, more_specs, aliases = [], [], {}
         ssq_shape, ssq_block = (rows, HD), lanes
     return pl.pallas_call(
-        functools.partial(residual_kernel, groups=groups, last=last),
+        functools.partial(residual_kernel, stages=stages, last=last),
         out_shape=[
             jax.ShapeDtypeStruct((rows, total_width), jnp.bfloat16),
             jax.ShapeDtypeStruct(ssq_shape, jnp.float32),
@@ -371,7 +363,7 @@
         compiler_params=pltpu.CompilerParams(vmem_limit_bytes=VMEM_LIMIT),
         cost_estimate=SMALL,
         name="residual",
-    )(where, hidden, *keeps, *recvs, *more)
+    )(where, hidden, *terms, *more)
 
 
 def join_kernel(*refs):
@@ -474,33 +466,31 @@
     out_pairs[1] = join(out_pairs[1], *in_pairs[-1])
     q, k, v = project_arrived(acc, done, rope, out_pairs[1][:1])
 
-    keeps, recvs = [], []
-
     def stage(s, attended, also=()):
         pieces = [p for pair in out_pairs[: last[s] + 1] for p in pair]
         return output_parts(choices[s], attended, pieces, n_tp, also)
 
-    def exchange(keep, send):
-        size, d = keep.shape[0], 1
-        while d < n_tp // 2:
-            received = swap(send, d)
-            size, d = size // 2, d * 2
-            total = [
-                (keep[i : i + 1].astype(jnp.float32) + received[i : i + 1].astype(jnp.float32)).astype(
-                    jnp.bfloat16
-                )
-                for i in range(2 * size)
-            ]
-            if d < n_tp // 2:
-                keep = jnp.concatenate(total[:size], 0)
-                send = jnp.concatenate(total[size:], 0)
-        keeps.extend(total[:size])
-        return total[size:]
-
-    def collect(raw):
-        sends = exchange(*raw)
-        recvs.extend(swap(part, n_tp // 2) for part in sends)
-        return sends
+    def exchange(parts):
+        d = 1
+        while True:
+            half = len(parts) // 2
+            received = [swap(part, d) for part in parts[half:]]
+            if half == 2:
+                return (parts[0], received[0]), (parts[1], received[1])
+            parts, d = [add(a, b) for a, b in zip(parts[:half], received)], d * 2
+
+    def add(a, b):
+        return (a.astype(jnp.float32) + b.astype(jnp.float32)).astype(jnp.bfloat16)
+
+    terms = []
+
+    def collect(parts, pieces=1):
+        stay, leave = exchange(parts)
+        share = rows // pieces
+        sends = [add(*(a[i : i + share] for a in leave)) for i in range(0, rows, share)]
+        recvs = [swap(part, n_tp // 2) for part in sends]
+        terms.append((*stay, recvs[0] if pieces == 1 else jnp.concatenate(recvs, axis=0)))
+        return sends, recvs
 
     shares = [0, 3, 6, 8]
     tq = rows // shares[-1]
@@ -518,32 +508,31 @@
             )
             waits = [attended]
         if flight > len(shares):
-            gates, sent = list(own), []
+            gates = list(own)
             if raw is not None:
-                gates, raw = gates + collect(raw), None
-                sent = recvs[-1:]
+                sends, waits = collect(raw)
+                gates, raw = gates + sends, None
             if last[pending[0]] < flight and len(pending) > 1:
                 raw = stage(pending.pop(0), attended, gates)
-                *arrived, passed = join((*arrived, raw[1]), *sent)
-                raw, waits = (raw[0], passed), []
+                half = len(raw) // 2
+                arrived = join((*arrived, *raw[half:]), *waits)
+                raw, arrived, waits = [*raw[:half], *arrived[2:]], arrived[:2], []
         out_pairs.append(join(arrived, *waits) if waits else tuple(arrived))
 
+    recvs = []
     while pending:
-        gates = collect(raw) if raw is not None else []
+        gates = []
+        if raw is not None:
+            gates, recvs = collect(raw, 2)
         raw = stage(pending.pop(0), attended, gates)
-    early = residual(where_early, hidden, keeps, recvs, width)
-    older = recvs[-1:]
-    keeps.clear()
-    recvs.clear()
-    keep, send = raw
-    (send,) = join((send,), *older)
-    collect((keep, send))
-    resid, ssq = residual(where_last, hidden, keeps, recvs, width, early)
-
-    d = 1
-    while d < n_tp:
-        ssq = ssq + swap(ssq, d)
-        d *= 2
+    early = residual(where_early, hidden, terms, width)
+    half = len(raw) // 2
+    raw = [*raw[:half], *join(raw[half:], *recvs[:1])]
+    collect(raw)
+    resid, ssq = residual(where_last, hidden, terms[-1:], width, early)
+
+    ssq = ssq[:1]
+    ssq = ssq + sum(swap(ssq, d) for d in range(1, n_tp))
     factor = lax.rsqrt(ssq[0] / model + norm_eps)
     normed = (resid.astype(jnp.float32) * factor[:, None] * gain[None, :]).astype(jnp.bfloat16)
     return (resid, normed)

time: 296 us -> 289 us (0.976)
  waiting for transfers between devices: 101 us -> 94.8 us
  Pallas kernels: 113 us -> 107 us
  starting transfers between devices: 39.1 us -> 43.3 us
    ppermute x13 -> x19, waiting for transfers between devices: 33.7 us -> 17.8 us  [body(): lax.ppermute(value, 'tp', [(i, i ^ d) for i in range(n_tp)])]
    ppermute x14, starting transfers between devices: 15.9 us -> 21.8 us  [body(): lax.ppermute(pair[0], 'rep', ahead)]
    pallas_call x3, Pallas kernels: 35.9 us -> 30.1 us  [attend(): pl.pallas_call(functools.partial(attend_kernel, first=first, heads=heads,...]
    ppermute x14, waiting for transfers between devices: 50.5 us -> 56 us  [body(): lax.ppermute(pair[0], 'rep', ahead)]
    ppermute x14, starting transfers between devices: 12.3 us -> 7.96 us  [body(): lax.ppermute(pair[1], 'rep', back)]
    ppermute x14, waiting for transfers between devices: 16.9 us -> 21 us  [body(): lax.ppermute(pair[1], 'rep', back)]
    ppermute x13 -> x19, starting transfers between devices: 10.9 us -> 13.5 us  [body(): lax.ppermute(value, 'tp', [(i, i ^ d) for i in range(n_tp)])]
    unnamed x48 -> x52, local copies, waits for them, and re-layouts: 6.12 us -> 5.26 us
  transfers between devices with their start and end apart: 41 -> 47, of which waited for: 31 -> 31; matrix products, arithmetic and copies ran while one was open for 8% -> 9% of each run, Pallas kernels for 37% -> 36%
where the time goes in v1:
time: 289 us; the launch traced here: 287 us
  Pallas kernels  107 us (37%)
  waiting for transfers between devices  94.8 us (33%)
  starting transfers between devices  43.3 us (15%)
  other arithmetic  25.3 us (9%)
  local copies, waits for them, and re-layouts  13.2 us (5%)
    ppermute x14, waiting for transfers between devices, body(): lax.ppermute(pair[0], 'rep', ahead)  56 us
    pallas_call x3, Pallas kernels, attend(): pl.pallas_call(functools.partial(attend_kernel, first=first, heads=heads,...  30.1 us
    pallas_call x3, Pallas kernels, project(): pl.pallas_call(kernel, out_shape=out_shape, grid_spec=pltpu.PrefetchScala...  29.6 us
    pallas_call x4, Pallas kernels, output_parts(): pl.pallas_call(skipping(kernel, 2 + count, len(also)), out_shape=[jax.Sha...  27.7 us
    ppermute x14, starting transfers between devices, body(): lax.ppermute(pair[0], 'rep', ahead)  21.8 us
    ppermute x14, waiting for transfers between devices, body(): lax.ppermute(pair[1], 'rep', back)  21 us
    ppermute x19, waiting for transfers between devices, body(): lax.ppermute(value, 'tp', [(i, i ^ d) for i in range(n_tp)])  17.8 us
    ppermute x19, starting transfers between devices, body(): lax.ppermute(value, 'tp', [(i, i ^ d) for i in range(n_tp)])  13.5 us
  transfers between devices with their start and end apart: 47, of which 31 were waited for; matrix products, arithmetic and copies ran while one was open for 9% of the time, Pallas kernels for 36%

profile of v1, /device:TPU:0, one launch (start us, length us, event | category | flops | bytes accessed | tf_op | source)
XLA Modules:
  0.0 286.9 jit_solution(10679075948416639763)
XLA Ops:
  14.9 6.1 %collective-permute-done.3.refs_2_.refs_0_ = bf16[1024,256]{1,0:T(8,128)(2,1)S(1)} collective-permute-done((bf16[1024,256]{1,0:T(8,128)(2,1)S(1)}, bf16[1024,256]{1,0:T(8,128)(2,1)S(1)}, u32[]{:S(2)}, u32[]{:S(2)}) %collective-permute-start.3) | collective-permute-done | bytes 524320 | tf_op jit(solution)/shard_map/ppermute | solution.py:399
  27.4 11.3 %collective-permute-done.5.refs_11_ = bf16[256,1280]{1,0:T(8,128)(2,1)} collective-permute-done((bf16[256,1280]{1,0:T(8,128)(2,1)}, bf16[256,1280]{1,0:T(8,128)(2,1)}, u32[]{:S(2)}, u32[]{:S(2)}) %collective-permute-start.5) | collective-permute-done | bytes 655392 | tf_op jit(solution)/shard_map/ppermute | solution.py:399
  42.8 3.2 %fusion.12 = (f32[1024,64]{1,0:T(8,128)}, f32[1024,64]{1,0:T(8,128)}, f32[1024,64]{1,0:T(8,128)}) fusion(f32[64]{0:T(128)S(1)} %negate_power_fusion, f32[1024]{0:T(1024)S(1)} %add_convert_fusion.5), kind=kLoop, calls=%fused_computation.33 | loop fusion | flops 131072 | bytes 790784 | tf_op jit(solution)/shard_map/neg | solution.py:62
  46.0 10.7 %input_norm.1.refs_2_.refs_1_.refs_3_.refs_4_.refs_5_.refs_6_.refs_7_.refs_8_ = bf16[1024,4096]{1,0:T(8,128)(2,1)} custom-call(bf16[1024,4096]{1,0:T(8,128)(2,1)} %h_ref.5, bf16[1,4096]{1,0:T(2,128)(2,1)} %reshape.112.gain_ref, bf16[256,1280]{1,0:T(8,128)(2,1)} %get-tuple-element.57.rest_0_.refs_9_), custom_call_target="tpu_custom_call" | custom-call | flops 1024 | bytes 1024 | tf_op jit(solution)/shard_map/input_norm/pallas_call | solution.py:90
  64.4 7.8 %collective-permute-done.10.refs_1_ = bf16[256,1280]{1,0:T(8,128)(2,1)S(1)} collective-permute-done((bf16[256,1280]{1,0:T(8,128)(2,1)}, bf16[256,1280]{1,0:T(8,128)(2,1)S(1)}, u32[]{:S(2)}, u32[]{:S(2)}) %collective-permute-start.10) | collective-permute-done | bytes 655392 | tf_op jit(solution)/shard_map/ppermute | solution.py:399
  75.9 11.3 %project.3.refs_2_.refs_9_ = f32[1024,1280]{1,0:T(8,128)} custom-call(s32[8]{0:T(128)} %slice_bitcast_fusion.1.refs_12_.refs_0_, bf16[1024,4096]{1,0:T(8,128)(2,1)} %input_norm.1.refs_2_.refs_1_.refs_3_.refs_4_.refs_5_.refs_6_.refs_7_.refs_8_, bf16[1024,4096]{1,0:T(8,128)(2,1)} %input_norm.1.refs_2_.refs_1_.refs_3_.refs_4_.refs_5_.refs_6_.refs_7_.refs_8_, ...), custom_call_target="tpu_custom_call" | custom-call | flops 1024 | bytes 1024 | tf_op jit(solution)/shard_map/project/pallas_call | solution.py:159
  90.6 12.9 %collective-permute-done.13.refs_7_ = bf16[256,1280]{1,0:T(8,128)(2,1)} collective-permute-done((bf16[256,1280]{1,0:T(8,128)(2,1)}, bf16[256,1280]{1,0:T(8,128)(2,1)}, u32[]{:S(2)}, u32[]{:S(2)}) %collective-permute-start.13) | collective-permute-done | bytes 655392 | tf_op jit(solution)/shard_map/ppermute | solution.py:399
  105.5 9.3 %project.4.refs_2_.refs_9_ = f32[1024,1280]{1,0:T(8,128)} custom-call(s32[4]{0:T(128)} %get-tuple-element.127.refs_13_.refs_0_, bf16[1024,4096]{1,0:T(8,128)(2,1)} %input_norm.1.refs_2_.refs_1_.refs_3_.refs_4_.refs_5_.refs_6_.refs_7_.refs_8_, bf16[1024,4096]{1,0:T(8,128)(2,1)} %input_norm.1.refs_2_.refs_1_.refs_3_.refs_4_.refs_5_.refs_6_.refs_7_.refs_8_, ...), custom_call_target="tpu_custom_call" | custom-call | flops 1024 | bytes 1024 | tf_op jit(solution)/shard_map/project/pallas_call | solution.py:159
  120.5 12.0 %collective-permute-done.17.refs_2_.refs_7_ = bf16[256,1280]{1,0:T(8,128)(2,1)S(1)} collective-permute-done((bf16[256,1280]{1,0:T(8,128)(2,1)}, bf16[256,1280]{1,0:T(8,128)(2,1)S(1)}, u32[]{:S(2)}, u32[]{:S(2)}) %collective-permute-start.17) | collective-permute-done | bytes 655392 | tf_op jit(solution)/shard_map/ppermute | solution.py:399
  135.3 8.9 %project.5 = (bf16[1024,1024]{1,0:T(8,128)(2,1)}, bf16[1024,128]{1,0:T(8,128)(2,1)}, bf16[1024,128]{1,0:T(8,128)(2,1)}) custom-call(s32[4]{0:T(128)} %get-tuple-element.128.refs_14_.refs_0_, bf16[1024,4096]{1,0:T(8,128)(2,1)} %input_norm.1.refs_2_.refs_1_.refs_3_.refs_4_.refs_5_.refs_6_.refs_7_.refs_8_, ...), custom_call_target="tpu_custom_call" | custom-call | flops 1024 | bytes 1024 | tf_op jit(solution)/shard_map/project/pallas_call | solution.py:159
  150.1 12.7 %attend.3.refs_2_.rest_0_ = bf16[1024,1024]{1,0:T(8,128)(2,1)} custom-call(s32[13]{0:T(128)} %pad_add_fusion.1.refs_2_.scal, bf16[1024,1024]{1,0:T(8,128)(2,1)} %get-tuple-element.68.refs_2_.q_ref, bf16[1024,128]{1,0:T(8,128)(2,1)} %get-tuple-element.69.k_ref, bf16[1024,128]{1,0:T(8,128)(2,1)} %get-tuple-element.70.v_ref, bf16[2048,1024]{1,0:T(8,128)(2,1)} %c_ref.5, ...), custom_call_target="tpu_custom_call" | custom-call | flops 1024 | bytes 1024 | tf_op jit(solution)/shard_map/attend/pallas_call | solution.py:227
  165.9 8.8 %attend.4.refs_2_.rest_0_ = bf16[1024,1024]{1,0:T(8,128)(2,1)} custom-call(s32[13]{0:T(128)} %pad_add_fusion.1.refs_2_.scal, bf16[1024,1024]{1,0:T(8,128)(2,1)} %get-tuple-element.68.refs_2_.q_ref, bf16[1024,128]{1,0:T(8,128)(2,1)} %get-tuple-element.69.k_ref, bf16[1024,128]{1,0:T(8,128)(2,1)} %get-tuple-element.70.v_ref, ...), custom_call_target="tpu_custom_call", output_to_operand_aliasing={{}: (5, {})} | custom-call | flops 1024 | bytes 1024 | tf_op jit(solution)/shard_map/attend/pallas_call | solution.py:227
  174.7 3.0 %collective-permute-done.23.refs_0_ = bf16[1024,256]{1,0:T(8,128)(2,1)S(1)} collective-permute-done((bf16[1024,256]{1,0:T(8,128)(2,1)}, bf16[1024,256]{1,0:T(8,128)(2,1)S(1)}, u32[]{:S(2)}, u32[]{:S(2)}) %collective-permute-start.23) | collective-permute-done | bytes 524320 | tf_op jit(solution)/shard_map/ppermute | solution.py:399
  182.0 8.6 %attend.5.refs_1_.refs_4_ = bf16[1024,1024]{1,0:T(8,128)(2,1)} custom-call(s32[13]{0:T(128)} %pad_add_fusion.1.refs_2_.scal, bf16[1024,1024]{1,0:T(8,128)(2,1)} %get-tuple-element.68.refs_2_.q_ref, bf16[1024,128]{1,0:T(8,128)(2,1)} %get-tuple-element.69.k_ref, bf16[1024,128]{1,0:T(8,128)(2,1)} %get-tuple-element.70.v_ref, ...), custom_call_target="tpu_custom_call", output_to_operand_aliasing={{}: (5, {})} | custom-call | flops 1024 | bytes 1024 | tf_op jit(solution)/shard_map/attend/pallas_call | solution.py:227
  190.5 6.9 %output_parts.4 = (bf16[1024,256]{1,0:T(8,128)(2,1)}, bf16[1024,256]{1,0:T(8,128)(2,1)}, bf16[1024,256]{1,0:T(8,128)(2,1)}, bf16[1024,256]{1,0:T(8,128)(2,1)}) custom-call(s32[4]{0:T(128)} %get-tuple-element.114.refs_5_.refs_0_, bf16[1024,1024]{1,0:T(8,128)(2,1)} %attend.5.refs_1_.refs_4_, bf16[1024,256]{1,0:T(8,128)(2,1)} %copy-done.7, ...), custom_call_target="tpu_custom_call" | custom-call | flops 1024 | bytes 1024 | tf_op jit(solution)/shard_map/output_parts/pallas_call | solution.py:284
  198.2 3.6 %collective-permute-start.27 = (bf16[1024,256]{1,0:T(8,128)(2,1)}, bf16[1024,256]{1,0:T(8,128)(2,1)S(1)}, u32[]{:S(2)}, u32[]{:S(2)}) collective-permute-start(bf16[1024,256]{1,0:T(8,128)(2,1)} %get-tuple-element.80.refs_12_), channel_id=1, source_target_pairs={{0,8},{8,16},{16,24},{24,28},{28,20},{20,12},{12,4},{4,0},{1,9},{9... | collective-permute-start | bytes 1572872 | tf_op jit(solution)/shard_map/ppermute | solution.py:399
  205.4 6.9 %output_parts.5 = (bf16[1024,256]{1,0:T(8,128)(2,1)}, bf16[1024,256]{1,0:T(8,128)(2,1)}, bf16[1024,256]{1,0:T(8,128)(2,1)}, bf16[1024,256]{1,0:T(8,128)(2,1)}) custom-call(s32[4]{0:T(128)} %get-tuple-element.113.refs_6_.refs_0_, bf16[1024,1024]{1,0:T(8,128)(2,1)} %attend.5.refs_1_.refs_4_, bf16[1024,256]{1,0:T(8,128)(2,1)} %copy-done.7, ...), custom_call_target="tpu_custom_call" | custom-call | flops 1024 | bytes 1024 | tf_op jit(solution)/shard_map/output_parts/pallas_call | solution.py:284
  223.8 6.9 %output_parts.6 = (bf16[1024,256]{1,0:T(8,128)(2,1)}, bf16[1024,256]{1,0:T(8,128)(2,1)}, bf16[1024,256]{1,0:T(8,128)(2,1)}, bf16[1024,256]{1,0:T(8,128)(2,1)}) custom-call(s32[4]{0:T(128)} %get-tuple-element.112.refs_7_.refs_0_, bf16[1024,1024]{1,0:T(8,128)(2,1)} %attend.5.refs_1_.refs_4_, bf16[1024,256]{1,0:T(8,128)(2,1)} %copy-done.7, ...), custom_call_target="tpu_custom_call" | custom-call | flops 1024 | bytes 1024 | tf_op jit(solution)/shard_map/output_parts/pallas_call | solution.py:284
  242.8 7.0 %output_parts.7 = (bf16[1024,256]{1,0:T(8,128)(2,1)}, bf16[1024,256]{1,0:T(8,128)(2,1)}, bf16[1024,256]{1,0:T(8,128)(2,1)}, bf16[1024,256]{1,0:T(8,128)(2,1)}) custom-call(s32[4]{0:T(128)} %get-tuple-element.115.refs_8_.refs_0_, bf16[1024,1024]{1,0:T(8,128)(2,1)} %attend.5.refs_1_.refs_4_, bf16[1024,256]{1,0:T(8,128)(2,1)} %copy-done.7, ...), custom_call_target="tpu_custom_call" | custom-call | flops 1024 | bytes 1024 | tf_op jit(solution)/shard_map/output_parts/pallas_call | solution.py:284
  255.5 4.3 %collective-permute-done.43 = bf16[512,256]{1,0:T(8,128)(2,1)S(1)} collective-permute-done((bf16[512,256]{1,0:T(8,128)(2,1)S(1)}, bf16[512,256]{1,0:T(8,128)(2,1)S(1)}, u32[]{:S(2)}, u32[]{:S(2)}) %collective-permute-start.43) | collective-permute-done | bytes 262176 | tf_op jit(solution)/shard_map/ppermute | solution.py:398
  262.9 5.6 %residual.2 = (bf16[1024,1024]{1,0:T(8,128)(2,1)}, f32[1024,128]{1,0:T(8,128)}) custom-call(s32[4]{0:T(128)} %pad_add_fusion.2.refs_9_.where, bf16[1024,4096]{1,0:T(8,128)(2,1)} %h_ref.5, bf16[1024,256]{1,0:T(8,128)(2,1)} %get-tuple-element.102.rest_0_, bf16[1024,256]{1,0:T(8,128)(2,1)} %collective-permute-done.40.rest_1_, ...), custom_call_target="tpu_custom_call" | custom-call | flops 1024 | bytes 1024 | tf_op jit(solution)/shard_map/residual/pallas_call | solution.py:350
  268.5 4.5 %collective-permute-done.39.rest_2_ = bf16[1024,256]{1,0:T(8,128)(2,1)S(1)} collective-permute-done((bf16[1024,256]{1,0:T(8,128)(2,1)}, bf16[1024,256]{1,0:T(8,128)(2,1)S(1)}, u32[]{:S(2)}, u32[]{:S(2)}) %collective-permute-start.39) | collective-permute-done | bytes 524320 | tf_op jit(solution)/shard_map/ppermute | solution.py:398
  273.8 3.7 %residual.3 = (bf16[1024,1024]{1,0:T(8,128)(2,1)}, f32[8,1024]{1,0:T(8,128)}) custom-call(s32[2]{0:T(128)} %pad_add_fusion.refs_10_.where, bf16[1024,4096]{1,0:T(8,128)(2,1)} %h_ref.5, bf16[1024,256]{1,0:T(8,128)(2,1)} %get-tuple-element.96.rest_0_, bf16[1024,256]{1,0:T(8,128)(2,1)} %collective-permute-done.37.rest_1_, ...), custom_call_target="tpu_custom_call", output_to_operand_aliasing={{0}: (5, {})} | custom-call | flops 1024 | bytes 1024 | tf_op jit(solution)/shard_map/residual/pallas_call | solution.py:350
  283.4 3.5 %multiply_convert_fusion = bf16[1024,1024]{1,0:T(8,128)(2,1)} fusion(bf16[1024,1024]{1,0:T(8,128)(2,1)} %get-tuple-element.55, f32[1024]{0:T(1024)S(1)} %copy-done.21, f32[1024]{0:T(1024)S(1)} %bitcast.35), kind=kLoop, calls=%fused_computation.1 | loop fusion | flops 4194304 | bytes 4202496 | tf_op jit(solution)/shard_map/convert_element_type | solution.py:537
  (192 shorter events, 105.6 us)
Async XLA Ops:
  6.9 14.1 %collective-permute-start.3 = (bf16[1024,256]{1,0:T(8,128)(2,1)S(1)}, bf16[1024,256]{1,0:T(8,128)(2,1)S(1)}, u32[]{:S(2)}, u32[]{:S(2)}) collective-permute-start(bf16[1024,256]{1,0:T(8,128)(2,1)S(1)} %get-tuple-element.123.refs_2_), channel_id=1, source_target_pairs={{0,8},{8,16},{16,24},{24,28},{28,20},{20,12},{12,4},{4,0},{1,9},{9... | collective-permute-start | bytes 1572872 | tf_op jit(solution)/shard_map/ppermute | solution.py:399
  8.7 14.0 %collective-permute-start.4 = (bf16[1024,256]{1,0:T(8,128)(2,1)S(1)}, bf16[1024,256]{1,0:T(8,128)(2,1)}, u32[]{:S(2)}, u32[]{:S(2)}) collective-permute-start(bf16[1024,256]{1,0:T(8,128)(2,1)S(1)} %get-tuple-element.122.refs_3_), channel_id=1, source_target_pairs={{8,0},{16,8},{24,16},{28,24},{20,28},{12,20},{4,12},{0,4},{9,1},{1... | collective-permute-start | bytes 1572872 | tf_op jit(solution)/shard_map/ppermute | solution.py:399
  22.6 16.2 %collective-permute-start.5 = (bf16[256,1280]{1,0:T(8,128)(2,1)}, bf16[256,1280]{1,0:T(8,128)(2,1)}, u32[]{:S(2)}, u32[]{:S(2)}) collective-permute-start(bf16[256,1280]{1,0:T(8,128)(2,1)} %get-tuple-element.57.rest_0_.refs_9_), channel_id=1, source_target_pairs={{0,8},{8,16},{16,24},{24,28},{28,20},{20,12},{12,4},{4,0},{1,9},{9... | collective-permute-start | bytes 1966088 | tf_op jit(solution)/shard_map/ppermute | solution.py:399
  24.2 16.2 %collective-permute-start.7 = (bf16[256,1280]{1,0:T(8,128)(2,1)}, bf16[256,1280]{1,0:T(8,128)(2,1)}, u32[]{:S(2)}, u32[]{:S(2)}) collective-permute-start(bf16[256,1280]{1,0:T(8,128)(2,1)} %get-tuple-element.58.refs_10_), channel_id=1, source_target_pairs={{8,0},{16,8},{24,16},{28,24},{20,28},{12,20},{4,12},{0,4},{9,1},{1... | collective-permute-start | bytes 1966088 | tf_op jit(solution)/shard_map/ppermute | solution.py:399
  38.8 18.0 %collective-permute-start.6 = (bf16[256,1280]{1,0:T(8,128)(2,1)}, bf16[256,1280]{1,0:T(8,128)(2,1)S(1)}, u32[]{:S(2)}, u32[]{:S(2)}) collective-permute-start(bf16[256,1280]{1,0:T(8,128)(2,1)} %collective-permute-done.5.refs_11_), channel_id=1, source_target_pairs={{0,8},{8,16},{16,24},{24,28},{28,20},{20,12},{12,4},{4,0},{1,9},{9... | collective-permute-start | bytes 1966088 | tf_op jit(solution)/shard_map/ppermute | solution.py:399
  40.4 16.4 %collective-permute-start.8 = (bf16[256,1280]{1,0:T(8,128)(2,1)}, bf16[256,1280]{1,0:T(8,128)(2,1)}, u32[]{:S(2)}, u32[]{:S(2)}) collective-permute-start(bf16[256,1280]{1,0:T(8,128)(2,1)} %collective-permute-done.7.refs_12_), channel_id=1, source_target_pairs={{8,0},{16,8},{24,16},{28,24},{20,28},{12,20},{4,12},{0,4},{9,1},{1... | collective-permute-start | bytes 1966088 | tf_op jit(solution)/shard_map/ppermute | solution.py:399
  57.6 14.6 %collective-permute-start.10 = (bf16[256,1280]{1,0:T(8,128)(2,1)}, bf16[256,1280]{1,0:T(8,128)(2,1)S(1)}, u32[]{:S(2)}, u32[]{:S(2)}) collective-permute-start(bf16[256,1280]{1,0:T(8,128)(2,1)} %get-tuple-element.60.refs_14_), channel_id=1, source_target_pairs={{8,0},{16,8},{24,16},{28,24},{20,28},{12,20},{4,12},{0,4},{9,1},{1... | collective-permute-start | bytes 1966088 | tf_op jit(solution)/shard_map/ppermute | solution.py:399
  58.9 14.9 %collective-permute-start.9 = (bf16[256,1280]{1,0:T(8,128)(2,1)}, bf16[256,1280]{1,0:T(8,128)(2,1)}, u32[]{:S(2)}, u32[]{:S(2)}) collective-permute-start(bf16[256,1280]{1,0:T(8,128)(2,1)} %get-tuple-element.59.refs_13_), channel_id=1, source_target_pairs={{0,8},{8,16},{16,24},{24,28},{28,20},{20,12},{12,4},{4,0},{1,9},{9... | collective-permute-start | bytes 1966088 | tf_op jit(solution)/shard_map/ppermute | solution.py:399
  73.8 14.0 %collective-permute-start.11 = (bf16[256,1280]{1,0:T(8,128)(2,1)}, bf16[256,1280]{1,0:T(8,128)(2,1)S(1)}, u32[]{:S(2)}, u32[]{:S(2)}) collective-permute-start(bf16[256,1280]{1,0:T(8,128)(2,1)} %get-tuple-element.61.refs_15_), channel_id=1, source_target_pairs={{0,8},{8,16},{16,24},{24,28},{28,20},{20,12},{12,4},{4,0},{1,9},{9... | collective-permute-start | bytes 1966088 | tf_op jit(solution)/shard_map/ppermute | solution.py:399
  88.6 14.9 %collective-permute-start.13 = (bf16[256,1280]{1,0:T(8,128)(2,1)}, bf16[256,1280]{1,0:T(8,128)(2,1)}, u32[]{:S(2)}, u32[]{:S(2)}) collective-permute-start(bf16[256,1280]{1,0:T(8,128)(2,1)} %get-tuple-element.63.refs_5_), channel_id=1, source_target_pairs={{0,8},{8,16},{16,24},{24,28},{28,20},{20,12},{12,4},{4,0},{1,9},{9... | collective-permute-start | bytes 1966088 | tf_op jit(solution)/shard_map/ppermute | solution.py:399
  89.8 14.9 %collective-permute-start.15 = (bf16[256,1280]{1,0:T(8,128)(2,1)}, bf16[256,1280]{1,0:T(8,128)(2,1)}, u32[]{:S(2)}, u32[]{:S(2)}) collective-permute-start(bf16[256,1280]{1,0:T(8,128)(2,1)} %get-tuple-element.64.refs_6_), channel_id=1, source_target_pairs={{8,0},{16,8},{24,16},{28,24},{20,28},{12,20},{4,12},{0,4},{9,1},{1... | collective-permute-start | bytes 1966088 | tf_op jit(solution)/shard_map/ppermute | solution.py:399
  118.4 14.0 %collective-permute-start.17 = (bf16[256,1280]{1,0:T(8,128)(2,1)}, bf16[256,1280]{1,0:T(8,128)(2,1)S(1)}, u32[]{:S(2)}, u32[]{:S(2)}) collective-permute-start(bf16[256,1280]{1,0:T(8,128)(2,1)} %get-tuple-element.65.refs_5_), channel_id=1, source_target_pairs={{0,8},{8,16},{16,24},{24,28},{28,20},{20,12},{12,4},{4,0},{1,9},{9... | collective-permute-start | bytes 1966088 | tf_op jit(solution)/shard_map/ppermute | solution.py:399
  148.1 14.7 %collective-permute-start.21 = (bf16[1024,256]{1,0:T(8,128)(2,1)}, bf16[1024,256]{1,0:T(8,128)(2,1)S(1)}, u32[]{:S(2)}, u32[]{:S(2)}) collective-permute-start(bf16[1024,256]{1,0:T(8,128)(2,1)} %get-tuple-element.72.rest_0_.refs_6_), channel_id=1, source_target_pairs={{0,8},{8,16},{16,24},{24,28},{28,20},{20,12},{12,4},{4,0},{1,9},{9... | collective-permute-start | bytes 1572872 | tf_op jit(solution)/shard_map/ppermute | solution.py:399
  149.7 14.1 %collective-permute-start.22 = (bf16[1024,256]{1,0:T(8,128)(2,1)}, bf16[1024,256]{1,0:T(8,128)(2,1)}, u32[]{:S(2)}, u32[]{:S(2)}) collective-permute-start(bf16[1024,256]{1,0:T(8,128)(2,1)} %get-tuple-element.73.refs_7_), channel_id=1, source_target_pairs={{8,0},{16,8},{24,16},{28,24},{20,28},{12,20},{4,12},{0,4},{9,1},{1... | collective-permute-start | bytes 1572872 | tf_op jit(solution)/shard_map/ppermute | solution.py:399
  165.3 14.6 %collective-permute-start.24 = (bf16[1024,256]{1,0:T(8,128)(2,1)}, bf16[1024,256]{1,0:T(8,128)(2,1)}, u32[]{:S(2)}, u32[]{:S(2)}) collective-permute-start(bf16[1024,256]{1,0:T(8,128)(2,1)} %get-tuple-element.75.refs_9_), channel_id=1, source_target_pairs={{8,0},{16,8},{24,16},{28,24},{20,28},{12,20},{4,12},{0,4},{9,1},{1... | collective-permute-start | bytes 1572872 | tf_op jit(solution)/shard_map/ppermute | solution.py:399
  179.9 17.5 %collective-permute-start.25 = (bf16[1024,256]{1,0:T(8,128)(2,1)}, bf16[1024,256]{1,0:T(8,128)(2,1)S(1)}, u32[]{:S(2)}, u32[]{:S(2)}) collective-permute-start(bf16[1024,256]{1,0:T(8,128)(2,1)} %get-tuple-element.76.rest_1_.refs_10_), channel_id=1, source_target_pairs={{0,8},{8,16},{16,24},{24,28},{28,20},{20,12},{12,4},{4,0},{1,9},{9... | collective-permute-start | bytes 1572872 | tf_op jit(solution)/shard_map/ppermute | solution.py:399
  181.0 16.5 %collective-permute-start.26 = (bf16[1024,256]{1,0:T(8,128)(2,1)}, bf16[1024,256]{1,0:T(8,128)(2,1)}, u32[]{:S(2)}, u32[]{:S(2)}) collective-permute-start(bf16[1024,256]{1,0:T(8,128)(2,1)} %get-tuple-element.77.refs_11_), channel_id=1, source_target_pairs={{8,0},{16,8},{24,16},{28,24},{20,28},{12,20},{4,12},{0,4},{9,1},{1... | collective-permute-start | bytes 1572872 | tf_op jit(solution)/shard_map/ppermute | solution.py:399
  198.2 16.1 %collective-permute-start.27 = (bf16[1024,256]{1,0:T(8,128)(2,1)}, bf16[1024,256]{1,0:T(8,128)(2,1)S(1)}, u32[]{:S(2)}, u32[]{:S(2)}) collective-permute-start(bf16[1024,256]{1,0:T(8,128)(2,1)} %get-tuple-element.80.refs_12_), channel_id=1, source_target_pairs={{0,8},{8,16},{16,24},{24,28},{28,20},{20,12},{12,4},{4,0},{1,9},{9... | collective-permute-start | bytes 1572872 | tf_op jit(solution)/shard_map/ppermute | solution.py:399
  201.8 14.4 %collective-permute-start.28 = (bf16[1024,256]{1,0:T(8,128)(2,1)}, bf16[1024,256]{1,0:T(8,128)(2,1)}, u32[]{:S(2)}, u32[]{:S(2)}) collective-permute-start(bf16[1024,256]{1,0:T(8,128)(2,1)} %get-tuple-element.81.refs_13_), channel_id=1, source_target_pairs={{8,0},{16,8},{24,16},{28,24},{20,28},{12,20},{4,12},{0,4},{9,1},{1... | collective-permute-start | bytes 1572872 | tf_op jit(solution)/shard_map/ppermute | solution.py:399
  203.8 14.4 %collective-permute-start.30 = (bf16[1024,256]{1,0:T(8,128)(2,1)}, bf16[1024,256]{1,0:T(8,128)(2,1)}, u32[]{:S(2)}, u32[]{:S(2)}) collective-permute-start(bf16[1024,256]{1,0:T(8,128)(2,1)} %add_convert_fusion.2.refs_13_), channel_id=1, source_target_pairs={{0,2},{1,3},{2,0},{3,1},{4,6},{5,7},{6,4},{7,5},{8,10},{9,11},{10,... | collective-permute-start | bytes 1572872 | tf_op jit(solution)/shard_map/ppermute | solution.py:398
  218.2 14.7 %collective-permute-start.31 = (bf16[1024,256]{1,0:T(8,128)(2,1)}, bf16[1024,256]{1,0:T(8,128)(2,1)}, u32[]{:S(2)}, u32[]{:S(2)}) collective-permute-start(bf16[1024,256]{1,0:T(8,128)(2,1)} %get-tuple-element.86.refs_14_.refs_16_), channel_id=1, source_target_pairs={{0,8},{8,16},{16,24},{24,28},{28,20},{20,12},{12,4},{4,0},{1,9},{9... | collective-permute-start | bytes 1572872 | tf_op jit(solution)/shard_map/ppermute | solution.py:399
  220.2 14.4 %collective-permute-start.32 = (bf16[1024,256]{1,0:T(8,128)(2,1)}, bf16[1024,256]{1,0:T(8,128)(2,1)}, u32[]{:S(2)}, u32[]{:S(2)}) collective-permute-start(bf16[1024,256]{1,0:T(8,128)(2,1)} %get-tuple-element.87.refs_15_), channel_id=1, source_target_pairs={{8,0},{16,8},{24,16},{28,24},{20,28},{12,20},{4,12},{0,4},{9,1},{1... | collective-permute-start | bytes 1572872 | tf_op jit(solution)/shard_map/ppermute | solution.py:399
  222.3 14.2 %collective-permute-start.34 = (bf16[1024,256]{1,0:T(8,128)(2,1)}, bf16[1024,256]{1,0:T(8,128)(2,1)S(1)}, u32[]{:S(2)}, u32[]{:S(2)}) collective-permute-start(bf16[1024,256]{1,0:T(8,128)(2,1)} %add_convert_fusion.1.refs_17_), channel_id=1, source_target_pairs={{0,2},{1,3},{2,0},{3,1},{4,6},{5,7},{6,4},{7,5},{8,10},{9,11},{10,... | collective-permute-start | bytes 1572872 | tf_op jit(solution)/shard_map/ppermute | solution.py:398
  253.4 15.1 %collective-permute-start.37 = (bf16[1024,256]{1,0:T(8,128)(2,1)}, bf16[1024,256]{1,0:T(8,128)(2,1)}, u32[]{:S(2)}, u32[]{:S(2)}) collective-permute-start(bf16[1024,256]{1,0:T(8,128)(2,1)} %get-tuple-element.99), channel_id=1, source_target_pairs={{0,1},{1,0},{2,3},{3,2},{4,5},{5,4},{6,7},{7,6},{8,9},{9,8},{10,11... | collective-permute-start | bytes 1572872 | tf_op jit(solution)/shard_map/ppermute | solution.py:398
  (49 other events, 333.6 us)

commit v2 on v1

--- a/solution.py
+++ b/solution.py
@@ -366,6 +366,39 @@
     )(where, hidden, *terms, *more)
 
 
+def output_norm_kernel(*refs, count, model):
+    squares, (r_ref, gain_ref, out_ref) = refs[:count], refs[count:]
+    total = lax.dot_general(
+        jnp.concatenate([ref[...] for ref in squares], axis=0),
+        jnp.ones((8 * count, HD), jnp.float32),
+        (((0,), (0,)), ((), ())),
+        precision=lax.Precision.HIGHEST,
+        preferred_element_type=jnp.float32,
+    )
+    factor = lax.rsqrt(total * (1.0 / (8 * model)) + norm_eps)
+    for i in range(0, r_ref.shape[1], HD):
+        at = slice(i, i + HD)
+        out_ref[:, at] = (r_ref[:, at].astype(jnp.float32) * factor * gain_ref[:, at]).astype(
+            jnp.bfloat16
+        )
+
+
+def output_norm(squares, resid, gain, model, tile=512):
+    rows, width = resid.shape
+    block = pl.BlockSpec((tile, width), lambda i: (i, 0))
+    return pl.pallas_call(
+        functools.partial(output_norm_kernel, count=len(squares), model=model),
+        out_shape=jax.ShapeDtypeStruct((rows, width), jnp.bfloat16),
+        grid=(rows // tile,),
+        in_specs=[pl.BlockSpec((8, tile), lambda i: (0, i))] * len(squares)
+        + [block, pl.BlockSpec((1, width), lambda i: (0, 0))],
+        out_specs=block,
+        compiler_params=pltpu.CompilerParams(vmem_limit_bytes=VMEM_LIMIT),
+        cost_estimate=SMALL,
+        name="output_norm",
+    )(*squares, resid, gain)
+
+
 def join_kernel(*refs):
     pass
 
@@ -436,7 +469,7 @@
     where_early = jnp.concatenate([column_all[:-1], tp[None]]).astype(jnp.int32)
     where_last = jnp.stack([column_all[-1], tp * halves + column_all[-1]]).astype(jnp.int32)
     width = model // n_tp
-    gain = lax.dynamic_slice_in_dim(out_gain, tp * width, width, 0).astype(jnp.float32)
+    gain = lax.dynamic_slice_in_dim(out_gain, tp * width, width, 0).astype(jnp.float32).reshape(1, width)
 
     first_cut, second_cut = n_rep // 2, n_rep - 2
     index = jnp.asarray(source)[rep]
@@ -466,18 +499,20 @@
     out_pairs[1] = join(out_pairs[1], *in_pairs[-1])
     q, k, v = project_arrived(acc, done, rope, out_pairs[1][:1])
 
-    def stage(s, attended, also=()):
-        pieces = [p for pair in out_pairs[: last[s] + 1] for p in pair]
-        return output_parts(choices[s], attended, pieces, n_tp, also)
-
-    def exchange(parts):
+    def stage(members, attended, also=()):
+        pieces = [p for pair in out_pairs[: last[members[-1]] + 1] for p in pair]
+        choice = jnp.stack([choices[s] for s in members], axis=1).reshape(-1)
+        return output_parts(choice, attended, pieces, choice.shape[0], also)
+
+    def exchange(parts, count):
         d = 1
         while True:
             half = len(parts) // 2
             received = [swap(part, d) for part in parts[half:]]
-            if half == 2:
-                return (parts[0], received[0]), (parts[1], received[1])
-            parts, d = [add(a, b) for a, b in zip(parts[:half], received)], d * 2
+            pairs = list(zip(parts[:half], received))
+            if half == 2 * count:
+                return pairs[:count], pairs[count:]
+            parts, d = [add(*pair) for pair in pairs], d * 2
 
     def add(a, b):
         return (a.astype(jnp.float32) + b.astype(jnp.float32)).astype(jnp.bfloat16)
@@ -485,16 +520,21 @@
     terms = []
 
     def collect(parts, pieces=1):
-        stay, leave = exchange(parts)
         share = rows // pieces
-        sends = [add(*(a[i : i + share] for a in leave)) for i in range(0, rows, share)]
-        recvs = [swap(part, n_tp // 2) for part in sends]
-        terms.append((*stay, recvs[0] if pieces == 1 else jnp.concatenate(recvs, axis=0)))
-        return sends, recvs
+        all_sends, all_recvs = [], []
+        for stay, leave in zip(*exchange(parts, len(parts) // n_tp)):
+            sends = [add(*(a[i : i + share] for a in leave)) for i in range(0, rows, share)]
+            recvs = [swap(part, n_tp // 2) for part in sends]
+            terms.append((*stay, recvs[0] if pieces == 1 else jnp.concatenate(recvs, axis=0)))
+            all_sends += sends
+            all_recvs += recvs
+        return all_sends, all_recvs
 
     shares = [0, 3, 6, 8]
     tq = rows // shares[-1]
-    attended, raw, pending = None, None, list(range(halves))
+    attended, raw, sent, pending = None, None, [], [[s] for s in range(halves)]
+    if halves > 3:
+        pending[:2] = [[0, 1]]
     for flight in range(2, n_rep):
         arrived = step(out_pairs[-1])
         own = list(out_pairs[-1][:1])
@@ -508,11 +548,13 @@
             )
             waits = [attended]
         if flight > len(shares):
-            gates = list(own)
+            gates = [*own, *sent[:1]]
+            waits += sent[1:]
+            sent = []
             if raw is not None:
-                sends, waits = collect(raw)
-                gates, raw = gates + sends, None
-            if last[pending[0]] < flight and len(pending) > 1:
+                sends, sent = collect(raw)
+                waits, raw = waits + sends, None
+            elif last[pending[0][-1]] < flight and len(pending) > 1:
                 raw = stage(pending.pop(0), attended, gates)
                 half = len(raw) // 2
                 arrived = join((*arrived, *raw[half:]), *waits)
@@ -531,10 +573,8 @@
     collect(raw)
     resid, ssq = residual(where_last, hidden, terms[-1:], width, early)
 
-    ssq = ssq[:1]
-    ssq = ssq + sum(swap(ssq, d) for d in range(1, n_tp))
-    factor = lax.rsqrt(ssq[0] / model + norm_eps)
-    normed = (resid.astype(jnp.float32) * factor[:, None] * gain[None, :]).astype(jnp.bfloat16)
+    squares = [ssq] + [swap(ssq, d) for d in range(1, n_tp)]
+    normed = output_norm(squares, resid, gain, model)
     return (resid, normed)
 
 

time: 289 us -> 286 us (0.990)
  other arithmetic: 25.3 us -> 21 us
    ppermute x14, waiting for transfers between devices: 56 us -> 61.8 us  [body(): lax.ppermute(pair[0], 'rep', ahead)]
    convert_element_type x2 -> x0, other arithmetic: 4.77 us -> none  [the longest x1 3.49 us: body(): (resid.astype(jnp.float32) * factor[:, None] * gain[None, :]).astype(jnp....]
    pallas_call x4 -> x3, Pallas kernels: 27.7 us -> 23.6 us  [output_parts(): pl.pallas_call(skipping(kernel, 2 + count, len(also)), out_shape=[jax.Sha...]
    pallas_call x0 -> x1, Pallas kernels: none -> 3.7 us  [output_norm(): pl.pallas_call(functools.partial(output_norm_kernel, count=len(squares),...]
    ppermute x19, waiting for transfers between devices: 17.8 us -> 14.6 us  [body(): lax.ppermute(value, 'tp', [(i, i ^ d) for i in range(n_tp)])]
    unnamed x52 -> x56, local copies, waits for them, and re-layouts: 5.26 us -> 5.99 us
  transfers between devices with their start and end apart: 47 -> 47, of which waited for: 31 -> 30; matrix products, arithmetic and copies ran while one was open for 9% -> 10% of each run, Pallas kernels for 36% -> 35%
where the time goes in v2:
time: 286 us; the launch traced here: 285 us
  Pallas kernels  106 us (37%)
  waiting for transfers between devices  96.6 us (34%)
  starting transfers between devices  44.4 us (16%)
  other arithmetic  21 us (7%)
  local copies, waits for them, and re-layouts  13.7 us (5%)
    ppermute x14, waiting for transfers between devices, body(): lax.ppermute(pair[0], 'rep', ahead)  61.8 us
    pallas_call x3, Pallas kernels, project(): pl.pallas_call(kernel, out_shape=out_shape, grid_spec=pltpu.PrefetchScala...  29.6 us
    pallas_call x3, Pallas kernels, attend(): pl.pallas_call(functools.partial(attend_kernel, first=first, heads=heads,...  29.5 us
    pallas_call x3, Pallas kernels, output_parts(): pl.pallas_call(skipping(kernel, 2 + count, len(also)), out_shape=[jax.Sha...  23.6 us
    ppermute x14, starting transfers between devices, body(): lax.ppermute(pair[0], 'rep', ahead)  21.8 us
    ppermute x14, waiting for transfers between devices, body(): lax.ppermute(pair[1], 'rep', back)  20.2 us
    ppermute x19, waiting for transfers between devices, body(): lax.ppermute(value, 'tp', [(i, i ^ d) for i in range(n_tp)])  14.6 us
    ppermute x19, starting transfers between devices, body(): lax.ppermute(value, 'tp', [(i, i ^ d) for i in range(n_tp)])  14.1 us
  transfers between devices with their start and end apart: 47, of which 30 were waited for; matrix products, arithmetic and copies ran while one was open for 10% of the time, Pallas kernels for 35%

profile of v2, /device:TPU:0, one launch (start us, length us, event | category | flops | bytes accessed | tf_op | source)
XLA Modules:
  0.0 284.8 jit_solution(11068506125753532550)
XLA Ops:
  14.8 6.2 %collective-permute-done.3.refs_2_.refs_0_ = bf16[1024,256]{1,0:T(8,128)(2,1)S(1)} collective-permute-done((bf16[1024,256]{1,0:T(8,128)(2,1)S(1)}, bf16[1024,256]{1,0:T(8,128)(2,1)S(1)}, u32[]{:S(2)}, u32[]{:S(2)}) %collective-permute-start.3) | collective-permute-done | bytes 524320 | tf_op jit(solution)/shard_map/ppermute | solution.py:432
  27.5 11.3 %collective-permute-done.5.refs_11_ = bf16[256,1280]{1,0:T(8,128)(2,1)} collective-permute-done((bf16[256,1280]{1,0:T(8,128)(2,1)}, bf16[256,1280]{1,0:T(8,128)(2,1)}, u32[]{:S(2)}, u32[]{:S(2)}) %collective-permute-start.5) | collective-permute-done | bytes 655392 | tf_op jit(solution)/shard_map/ppermute | solution.py:432
  42.8 3.2 %fusion.12 = (f32[1024,64]{1,0:T(8,128)}, f32[1024,64]{1,0:T(8,128)}, f32[1024,64]{1,0:T(8,128)}) fusion(f32[64]{0:T(128)S(1)} %negate_power_fusion, f32[1024]{0:T(1024)S(1)} %add_convert_fusion.5), kind=kLoop, calls=%fused_computation.32 | loop fusion | flops 131072 | bytes 790784 | tf_op jit(solution)/shard_map/neg | solution.py:62
  46.0 10.7 %input_norm.1.refs_2_.refs_1_.refs_3_.refs_4_.refs_5_.refs_6_.refs_7_.refs_8_ = bf16[1024,4096]{1,0:T(8,128)(2,1)} custom-call(bf16[1024,4096]{1,0:T(8,128)(2,1)} %h_ref.5, bf16[1,4096]{1,0:T(2,128)(2,1)} %reshape.107.gain_ref, bf16[256,1280]{1,0:T(8,128)(2,1)} %get-tuple-element.57.rest_0_.refs_9_), custom_call_target="tpu_custom_call" | custom-call | flops 1024 | bytes 1024 | tf_op jit(solution)/shard_map/input_norm/pallas_call | solution.py:90
  64.3 7.9 %collective-permute-done.10.refs_1_ = bf16[256,1280]{1,0:T(8,128)(2,1)S(1)} collective-permute-done((bf16[256,1280]{1,0:T(8,128)(2,1)}, bf16[256,1280]{1,0:T(8,128)(2,1)S(1)}, u32[]{:S(2)}, u32[]{:S(2)}) %collective-permute-start.10) | collective-permute-done | bytes 655392 | tf_op jit(solution)/shard_map/ppermute | solution.py:432
  75.8 11.3 %project.3.refs_2_.refs_9_ = f32[1024,1280]{1,0:T(8,128)} custom-call(s32[8]{0:T(128)} %slice_bitcast_fusion.1.refs_12_.refs_0_, bf16[1024,4096]{1,0:T(8,128)(2,1)} %input_norm.1.refs_2_.refs_1_.refs_3_.refs_4_.refs_5_.refs_6_.refs_7_.refs_8_, bf16[1024,4096]{1,0:T(8,128)(2,1)} %input_norm.1.refs_2_.refs_1_.refs_3_.refs_4_.refs_5_.refs_6_.refs_7_.refs_8_, ...), custom_call_target="tpu_custom_call" | custom-call | flops 1024 | bytes 1024 | tf_op jit(solution)/shard_map/project/pallas_call | solution.py:159
  90.6 12.9 %collective-permute-done.13.refs_7_ = bf16[256,1280]{1,0:T(8,128)(2,1)} collective-permute-done((bf16[256,1280]{1,0:T(8,128)(2,1)}, bf16[256,1280]{1,0:T(8,128)(2,1)}, u32[]{:S(2)}, u32[]{:S(2)}) %collective-permute-start.13) | collective-permute-done | bytes 655392 | tf_op jit(solution)/shard_map/ppermute | solution.py:432
  105.5 9.3 %project.4.refs_2_.refs_9_ = f32[1024,1280]{1,0:T(8,128)} custom-call(s32[4]{0:T(128)} %get-tuple-element.127.refs_13_.refs_0_, bf16[1024,4096]{1,0:T(8,128)(2,1)} %input_norm.1.refs_2_.refs_1_.refs_3_.refs_4_.refs_5_.refs_6_.refs_7_.refs_8_, bf16[1024,4096]{1,0:T(8,128)(2,1)} %input_norm.1.refs_2_.refs_1_.refs_3_.refs_4_.refs_5_.refs_6_.refs_7_.refs_8_, ...), custom_call_target="tpu_custom_call" | custom-call | flops 1024 | bytes 1024 | tf_op jit(solution)/shard_map/project/pallas_call | solution.py:159
  120.4 12.0 %collective-permute-done.17.refs_2_.refs_7_ = bf16[256,1280]{1,0:T(8,128)(2,1)S(1)} collective-permute-done((bf16[256,1280]{1,0:T(8,128)(2,1)}, bf16[256,1280]{1,0:T(8,128)(2,1)S(1)}, u32[]{:S(2)}, u32[]{:S(2)}) %collective-permute-start.17) | collective-permute-done | bytes 655392 | tf_op jit(solution)/shard_map/ppermute | solution.py:432
  135.3 8.9 %project.5 = (bf16[1024,1024]{1,0:T(8,128)(2,1)}, bf16[1024,128]{1,0:T(8,128)(2,1)}, bf16[1024,128]{1,0:T(8,128)(2,1)}) custom-call(s32[4]{0:T(128)} %get-tuple-element.128.refs_14_.refs_0_, bf16[1024,4096]{1,0:T(8,128)(2,1)} %input_norm.1.refs_2_.refs_1_.refs_3_.refs_4_.refs_5_.refs_6_.refs_7_.refs_8_, ...), custom_call_target="tpu_custom_call" | custom-call | flops 1024 | bytes 1024 | tf_op jit(solution)/shard_map/project/pallas_call | solution.py:159
  150.1 10.8 %attend.3.refs_2_.rest_0_ = bf16[1024,1024]{1,0:T(8,128)(2,1)} custom-call(s32[13]{0:T(128)} %pad_add_fusion.1.refs_2_.scal, bf16[1024,1024]{1,0:T(8,128)(2,1)} %get-tuple-element.68.refs_2_.q_ref, bf16[1024,128]{1,0:T(8,128)(2,1)} %get-tuple-element.69.k_ref, bf16[1024,128]{1,0:T(8,128)(2,1)} %get-tuple-element.70.v_ref, bf16[2048,1024]{1,0:T(8,128)(2,1)} %c_ref.5, ...), custom_call_target="tpu_custom_call" | custom-call | flops 1024 | bytes 1024 | tf_op jit(solution)/shard_map/attend/pallas_call | solution.py:227
  161.9 4.0 %collective-permute-start.23 = (bf16[1024,256]{1,0:T(8,128)(2,1)}, bf16[1024,256]{1,0:T(8,128)(2,1)S(1)}, u32[]{:S(2)}, u32[]{:S(2)}) collective-permute-start(bf16[1024,256]{1,0:T(8,128)(2,1)} %get-tuple-element.74.rest_1_.refs_8_), channel_id=1, source_target_pairs={{0,8},{8,16},{16,24},{24,28},{28,20},{20,12},{12,4},{4,0},{1,9},{9... | collective-permute-start | bytes 1572872 | tf_op jit(solution)/shard_map/ppermute | solution.py:432
  165.9 8.8 %attend.4.refs_2_.rest_0_ = bf16[1024,1024]{1,0:T(8,128)(2,1)} custom-call(s32[13]{0:T(128)} %pad_add_fusion.1.refs_2_.scal, bf16[1024,1024]{1,0:T(8,128)(2,1)} %get-tuple-element.68.refs_2_.q_ref, bf16[1024,128]{1,0:T(8,128)(2,1)} %get-tuple-element.69.k_ref, bf16[1024,128]{1,0:T(8,128)(2,1)} %get-tuple-element.70.v_ref, ...), custom_call_target="tpu_custom_call", output_to_operand_aliasing={{}: (5, {})} | custom-call | flops 1024 | bytes 1024 | tf_op jit(solution)/shard_map/attend/pallas_call | solution.py:227
  174.7 3.8 %collective-permute-done.23.refs_0_ = bf16[1024,256]{1,0:T(8,128)(2,1)S(1)} collective-permute-done((bf16[1024,256]{1,0:T(8,128)(2,1)}, bf16[1024,256]{1,0:T(8,128)(2,1)S(1)}, u32[]{:S(2)}, u32[]{:S(2)}) %collective-permute-start.23) | collective-permute-done | bytes 524320 | tf_op jit(solution)/shard_map/ppermute | solution.py:432
  183.4 9.8 %attend.5.refs_1_.refs_6_ = bf16[1024,1024]{1,0:T(8,128)(2,1)} custom-call(s32[13]{0:T(128)} %pad_add_fusion.1.refs_2_.scal, bf16[1024,1024]{1,0:T(8,128)(2,1)} %get-tuple-element.68.refs_2_.q_ref, bf16[1024,128]{1,0:T(8,128)(2,1)} %get-tuple-element.69.k_ref, bf16[1024,128]{1,0:T(8,128)(2,1)} %get-tuple-element.70.v_ref, ...), custom_call_target="tpu_custom_call", output_to_operand_aliasing={{}: (5, {})} | custom-call | flops 1024 | bytes 1024 | tf_op jit(solution)/shard_map/attend/pallas_call | solution.py:227
  193.2 9.7 %output_parts.3 = (bf16[1024,256]{1,0:T(8,128)(2,1)}, bf16[1024,256]{1,0:T(8,128)(2,1)}, bf16[1024,256]{1,0:T(8,128)(2,1)}, bf16[1024,256]{1,0:T(8,128)(2,1)}, b...) custom-call(s32[8]{0:T(128)} %reshape.110.refs_0_, ...), custom_call_target="tpu_custom_call" | custom-call | flops 1024 | bytes 1024 | tf_op jit(solution)/shard_map/output_parts/pallas_call | solution.py:284
  212.0 6.4 %collective-permute-done.27.refs_0_ = bf16[1024,256]{1,0:T(8,128)(2,1)S(1)} collective-permute-done((bf16[1024,256]{1,0:T(8,128)(2,1)}, bf16[1024,256]{1,0:T(8,128)(2,1)S(1)}, u32[]{:S(2)}, u32[]{:S(2)}) %collective-permute-start.27) | collective-permute-done | bytes 524320 | tf_op jit(solution)/shard_map/ppermute | solution.py:432
  223.9 6.9 %output_parts.4 = (bf16[1024,256]{1,0:T(8,128)(2,1)}, bf16[1024,256]{1,0:T(8,128)(2,1)}, bf16[1024,256]{1,0:T(8,128)(2,1)}, bf16[1024,256]{1,0:T(8,128)(2,1)}) custom-call(s32[4]{0:T(128)} %get-tuple-element.112.refs_7_.refs_0_, bf16[1024,1024]{1,0:T(8,128)(2,1)} %attend.5.refs_1_.refs_6_, bf16[1024,256]{1,0:T(8,128)(2,1)} %copy-done.7, ...), custom_call_target="tpu_custom_call" | custom-call | flops 1024 | bytes 1024 | tf_op jit(solution)/shard_map/output_parts/pallas_call | solution.py:284
  241.0 7.0 %output_parts.5 = (bf16[1024,256]{1,0:T(8,128)(2,1)}, bf16[1024,256]{1,0:T(8,128)(2,1)}, bf16[1024,256]{1,0:T(8,128)(2,1)}, bf16[1024,256]{1,0:T(8,128)(2,1)}) custom-call(s32[4]{0:T(128)} %get-tuple-element.115.refs_8_.refs_0_, bf16[1024,1024]{1,0:T(8,128)(2,1)} %attend.5.refs_1_.refs_6_, bf16[1024,256]{1,0:T(8,128)(2,1)} %copy-done.7, ...), custom_call_target="tpu_custom_call" | custom-call | flops 1024 | bytes 1024 | tf_op jit(solution)/shard_map/output_parts/pallas_call | solution.py:284
  253.7 4.3 %collective-permute-done.43 = bf16[512,256]{1,0:T(8,128)(2,1)S(1)} collective-permute-done((bf16[512,256]{1,0:T(8,128)(2,1)S(1)}, bf16[512,256]{1,0:T(8,128)(2,1)S(1)}, u32[]{:S(2)}, u32[]{:S(2)}) %collective-permute-start.43) | collective-permute-done | bytes 262176 | tf_op jit(solution)/shard_map/ppermute | solution.py:431
  261.1 5.6 %residual.2 = (bf16[1024,1024]{1,0:T(8,128)(2,1)}, f32[1024,128]{1,0:T(8,128)}) custom-call(s32[4]{0:T(128)} %pad_add_fusion.2.refs_9_.where, bf16[1024,4096]{1,0:T(8,128)(2,1)} %h_ref.5, bf16[1024,256]{1,0:T(8,128)(2,1)} %get-tuple-element.102.rest_0_, bf16[1024,256]{1,0:T(8,128)(2,1)} %collective-permute-done.40.rest_1_, ...), custom_call_target="tpu_custom_call" | custom-call | flops 1024 | bytes 1024 | tf_op jit(solution)/shard_map/residual/pallas_call | solution.py:350
  266.7 4.4 %collective-permute-done.39.rest_2_ = bf16[1024,256]{1,0:T(8,128)(2,1)S(1)} collective-permute-done((bf16[1024,256]{1,0:T(8,128)(2,1)}, bf16[1024,256]{1,0:T(8,128)(2,1)S(1)}, u32[]{:S(2)}, u32[]{:S(2)}) %collective-permute-start.39) | collective-permute-done | bytes 524320 | tf_op jit(solution)/shard_map/ppermute | solution.py:431
  272.0 3.6 %residual.3 = (bf16[1024,1024]{1,0:T(8,128)(2,1)}, f32[8,1024]{1,0:T(8,128)}) custom-call(s32[2]{0:T(128)} %pad_add_fusion.refs_10_.where, bf16[1024,4096]{1,0:T(8,128)(2,1)} %h_ref.5, bf16[1024,256]{1,0:T(8,128)(2,1)} %get-tuple-element.96.rest_0_, bf16[1024,256]{1,0:T(8,128)(2,1)} %collective-permute-done.37.rest_1_, ...), custom_call_target="tpu_custom_call", output_to_operand_aliasing={{0}: (5, {})} | custom-call | flops 1024 | bytes 1024 | tf_op jit(solution)/shard_map/residual/pallas_call | solution.py:350
  281.1 3.7 %output_norm.1 = bf16[1024,1024]{1,0:T(8,128)(2,1)} custom-call(f32[8,1024]{1,0:T(8,128)} %get-tuple-element.111.refs_0_, f32[8,1024]{1,0:T(8,128)} %copy-done.21, f32[8,1024]{1,0:T(8,128)} %copy-done.22, f32[8,1024]{1,0:T(8,128)} %copy-done.23, bf16[1024,1024]{1,0:T(8,128)(2,1)} %get-tuple-element.55.refs_4_, f32[1,1024]{1,0:T(1,128)} %bitcast.38), custom_call_target="tpu_custom_call" | custom-call | flops 1024 | bytes 1024 | tf_op jit(solution)/shard_map/output_norm/pallas_call | solution.py:389
  (194 shorter events, 100.6 us)
Async XLA Ops:
  6.9 14.1 %collective-permute-start.3 = (bf16[1024,256]{1,0:T(8,128)(2,1)S(1)}, bf16[1024,256]{1,0:T(8,128)(2,1)S(1)}, u32[]{:S(2)}, u32[]{:S(2)}) collective-permute-start(bf16[1024,256]{1,0:T(8,128)(2,1)S(1)} %get-tuple-element.123.refs_2_), channel_id=1, source_target_pairs={{0,8},{8,16},{16,24},{24,28},{28,20},{20,12},{12,4},{4,0},{1,9},{9... | collective-permute-start | bytes 1572872 | tf_op jit(solution)/shard_map/ppermute | solution.py:432
  8.7 14.0 %collective-permute-start.4 = (bf16[1024,256]{1,0:T(8,128)(2,1)S(1)}, bf16[1024,256]{1,0:T(8,128)(2,1)}, u32[]{:S(2)}, u32[]{:S(2)}) collective-permute-start(bf16[1024,256]{1,0:T(8,128)(2,1)S(1)} %get-tuple-element.122.refs_3_), channel_id=1, source_target_pairs={{8,0},{16,8},{24,16},{28,24},{20,28},{12,20},{4,12},{0,4},{9,1},{1... | collective-permute-start | bytes 1572872 | tf_op jit(solution)/shard_map/ppermute | solution.py:432
  22.6 16.2 %collective-permute-start.5 = (bf16[256,1280]{1,0:T(8,128)(2,1)}, bf16[256,1280]{1,0:T(8,128)(2,1)}, u32[]{:S(2)}, u32[]{:S(2)}) collective-permute-start(bf16[256,1280]{1,0:T(8,128)(2,1)} %get-tuple-element.57.rest_0_.refs_9_), channel_id=1, source_target_pairs={{0,8},{8,16},{16,24},{24,28},{28,20},{20,12},{12,4},{4,0},{1,9},{9... | collective-permute-start | bytes 1966088 | tf_op jit(solution)/shard_map/ppermute | solution.py:432
  24.2 16.2 %collective-permute-start.7 = (bf16[256,1280]{1,0:T(8,128)(2,1)}, bf16[256,1280]{1,0:T(8,128)(2,1)}, u32[]{:S(2)}, u32[]{:S(2)}) collective-permute-start(bf16[256,1280]{1,0:T(8,128)(2,1)} %get-tuple-element.58.refs_10_), channel_id=1, source_target_pairs={{8,0},{16,8},{24,16},{28,24},{20,28},{12,20},{4,12},{0,4},{9,1},{1... | collective-permute-start | bytes 1966088 | tf_op jit(solution)/shard_map/ppermute | solution.py:432
  38.8 17.9 %collective-permute-start.6 = (bf16[256,1280]{1,0:T(8,128)(2,1)}, bf16[256,1280]{1,0:T(8,128)(2,1)S(1)}, u32[]{:S(2)}, u32[]{:S(2)}) collective-permute-start(bf16[256,1280]{1,0:T(8,128)(2,1)} %collective-permute-done.5.refs_11_), channel_id=1, source_target_pairs={{0,8},{8,16},{16,24},{24,28},{28,20},{20,12},{12,4},{4,0},{1,9},{9... | collective-permute-start | bytes 1966088 | tf_op jit(solution)/shard_map/ppermute | solution.py:432
  40.4 16.4 %collective-permute-start.8 = (bf16[256,1280]{1,0:T(8,128)(2,1)}, bf16[256,1280]{1,0:T(8,128)(2,1)}, u32[]{:S(2)}, u32[]{:S(2)}) collective-permute-start(bf16[256,1280]{1,0:T(8,128)(2,1)} %collective-permute-done.7.refs_12_), channel_id=1, source_target_pairs={{8,0},{16,8},{24,16},{28,24},{20,28},{12,20},{4,12},{0,4},{9,1},{1... | collective-permute-start | bytes 1966088 | tf_op jit(solution)/shard_map/ppermute | solution.py:432
  57.6 14.6 %collective-permute-start.10 = (bf16[256,1280]{1,0:T(8,128)(2,1)}, bf16[256,1280]{1,0:T(8,128)(2,1)S(1)}, u32[]{:S(2)}, u32[]{:S(2)}) collective-permute-start(bf16[256,1280]{1,0:T(8,128)(2,1)} %get-tuple-element.60.refs_14_), channel_id=1, source_target_pairs={{8,0},{16,8},{24,16},{28,24},{20,28},{12,20},{4,12},{0,4},{9,1},{1... | collective-permute-start | bytes 1966088 | tf_op jit(solution)/shard_map/ppermute | solution.py:432
  58.9 14.9 %collective-permute-start.9 = (bf16[256,1280]{1,0:T(8,128)(2,1)}, bf16[256,1280]{1,0:T(8,128)(2,1)}, u32[]{:S(2)}, u32[]{:S(2)}) collective-permute-start(bf16[256,1280]{1,0:T(8,128)(2,1)} %get-tuple-element.59.refs_13_), channel_id=1, source_target_pairs={{0,8},{8,16},{16,24},{24,28},{28,20},{20,12},{12,4},{4,0},{1,9},{9... | collective-permute-start | bytes 1966088 | tf_op jit(solution)/shard_map/ppermute | solution.py:432
  73.8 14.0 %collective-permute-start.11 = (bf16[256,1280]{1,0:T(8,128)(2,1)}, bf16[256,1280]{1,0:T(8,128)(2,1)S(1)}, u32[]{:S(2)}, u32[]{:S(2)}) collective-permute-start(bf16[256,1280]{1,0:T(8,128)(2,1)} %get-tuple-element.61.refs_15_), channel_id=1, source_target_pairs={{0,8},{8,16},{16,24},{24,28},{28,20},{20,12},{12,4},{4,0},{1,9},{9... | collective-permute-start | bytes 1966088 | tf_op jit(solution)/shard_map/ppermute | solution.py:432
  74.6 13.6 %collective-permute-start.12 = (bf16[256,1280]{1,0:T(8,128)(2,1)}, bf16[256,1280]{1,0:T(8,128)(2,1)}, u32[]{:S(2)}, u32[]{:S(2)}) collective-permute-start(bf16[256,1280]{1,0:T(8,128)(2,1)} %get-tuple-element.62.refs_16_), channel_id=1, source_target_pairs={{8,0},{16,8},{24,16},{28,24},{20,28},{12,20},{4,12},{0,4},{9,1},{1... | collective-permute-start | bytes 1966088 | tf_op jit(solution)/shard_map/ppermute | solution.py:432
  88.6 14.9 %collective-permute-start.13 = (bf16[256,1280]{1,0:T(8,128)(2,1)}, bf16[256,1280]{1,0:T(8,128)(2,1)}, u32[]{:S(2)}, u32[]{:S(2)}) collective-permute-start(bf16[256,1280]{1,0:T(8,128)(2,1)} %get-tuple-element.63.refs_5_), channel_id=1, source_target_pairs={{0,8},{8,16},{16,24},{24,28},{28,20},{20,12},{12,4},{4,0},{1,9},{9... | collective-permute-start | bytes 1966088 | tf_op jit(solution)/shard_map/ppermute | solution.py:432
  89.8 14.9 %collective-permute-start.15 = (bf16[256,1280]{1,0:T(8,128)(2,1)}, bf16[256,1280]{1,0:T(8,128)(2,1)}, u32[]{:S(2)}, u32[]{:S(2)}) collective-permute-start(bf16[256,1280]{1,0:T(8,128)(2,1)} %get-tuple-element.64.refs_6_), channel_id=1, source_target_pairs={{8,0},{16,8},{24,16},{28,24},{20,28},{12,20},{4,12},{0,4},{9,1},{1... | collective-permute-start | bytes 1966088 | tf_op jit(solution)/shard_map/ppermute | solution.py:432
  103.5 13.9 %collective-permute-start.14 = (bf16[256,1280]{1,0:T(8,128)(2,1)}, bf16[256,1280]{1,0:T(8,128)(2,1)S(1)}, u32[]{:S(2)}, u32[]{:S(2)}) collective-permute-start(bf16[256,1280]{1,0:T(8,128)(2,1)} %collective-permute-done.13.refs_7_), channel_id=1, source_target_pairs={{0,8},{8,16},{16,24},{24,28},{28,20},{20,12},{12,4},{4,0},{1,9},{9... | collective-permute-start | bytes 1966088 | tf_op jit(solution)/shard_map/ppermute | solution.py:432
  104.7 13.7 %collective-permute-start.16 = (bf16[256,1280]{1,0:T(8,128)(2,1)}, bf16[256,1280]{1,0:T(8,128)(2,1)}, u32[]{:S(2)}, u32[]{:S(2)}) collective-permute-start(bf16[256,1280]{1,0:T(8,128)(2,1)} %collective-permute-done.15.refs_8_), channel_id=1, source_target_pairs={{8,0},{16,8},{24,16},{28,24},{20,28},{12,20},{4,12},{0,4},{9,1},{1... | collective-permute-start | bytes 1966088 | tf_op jit(solution)/shard_map/ppermute | solution.py:432
  118.4 14.0 %collective-permute-start.17 = (bf16[256,1280]{1,0:T(8,128)(2,1)}, bf16[256,1280]{1,0:T(8,128)(2,1)S(1)}, u32[]{:S(2)}, u32[]{:S(2)}) collective-permute-start(bf16[256,1280]{1,0:T(8,128)(2,1)} %get-tuple-element.65.refs_5_), channel_id=1, source_target_pairs={{0,8},{8,16},{16,24},{24,28},{28,20},{20,12},{12,4},{4,0},{1,9},{9... | collective-permute-start | bytes 1966088 | tf_op jit(solution)/shard_map/ppermute | solution.py:432
  161.9 16.6 %collective-permute-start.23 = (bf16[1024,256]{1,0:T(8,128)(2,1)}, bf16[1024,256]{1,0:T(8,128)(2,1)S(1)}, u32[]{:S(2)}, u32[]{:S(2)}) collective-permute-start(bf16[1024,256]{1,0:T(8,128)(2,1)} %get-tuple-element.74.rest_1_.refs_8_), channel_id=1, source_target_pairs={{0,8},{8,16},{16,24},{24,28},{28,20},{20,12},{12,4},{4,0},{1,9},{9... | collective-permute-start | bytes 1572872 | tf_op jit(solution)/shard_map/ppermute | solution.py:432
  165.9 14.9 %collective-permute-start.24 = (bf16[1024,256]{1,0:T(8,128)(2,1)}, bf16[1024,256]{1,0:T(8,128)(2,1)}, u32[]{:S(2)}, u32[]{:S(2)}) collective-permute-start(bf16[1024,256]{1,0:T(8,128)(2,1)} %get-tuple-element.75.refs_9_), channel_id=1, source_target_pairs={{8,0},{16,8},{24,16},{28,24},{20,28},{12,20},{4,12},{0,4},{9,1},{1... | collective-permute-start | bytes 1572872 | tf_op jit(solution)/shard_map/ppermute | solution.py:432
  180.8 22.2 %collective-permute-start.25 = (bf16[1024,256]{1,0:T(8,128)(2,1)}, bf16[1024,256]{1,0:T(8,128)(2,1)S(1)}, u32[]{:S(2)}, u32[]{:S(2)}) collective-permute-start(bf16[1024,256]{1,0:T(8,128)(2,1)} %get-tuple-element.76.rest_1_.refs_10_.refs_12_), channel_id=1, source_target_pairs={{0,8},{8,16},{16,24},{24,28},{28,20},{20,12},{12,4},{4,0},{1,9},{9... | collective-permute-start | bytes 1572872 | tf_op jit(solution)/shard_map/ppermute | solution.py:432
  181.7 21.3 %collective-permute-start.26 = (bf16[1024,256]{1,0:T(8,128)(2,1)}, bf16[1024,256]{1,0:T(8,128)(2,1)}, u32[]{:S(2)}, u32[]{:S(2)}) collective-permute-start(bf16[1024,256]{1,0:T(8,128)(2,1)} %get-tuple-element.77.refs_11_), channel_id=1, source_target_pairs={{8,0},{16,8},{24,16},{28,24},{20,28},{12,20},{4,12},{0,4},{9,1},{1... | collective-permute-start | bytes 1572872 | tf_op jit(solution)/shard_map/ppermute | solution.py:432
  204.3 14.0 %collective-permute-start.27 = (bf16[1024,256]{1,0:T(8,128)(2,1)}, bf16[1024,256]{1,0:T(8,128)(2,1)S(1)}, u32[]{:S(2)}, u32[]{:S(2)}) collective-permute-start(bf16[1024,256]{1,0:T(8,128)(2,1)} %get-tuple-element.82.refs_12_), channel_id=1, source_target_pairs={{0,8},{8,16},{16,24},{24,28},{28,20},{20,12},{12,4},{4,0},{1,9},{9... | collective-permute-start | bytes 1572872 | tf_op jit(solution)/shard_map/ppermute | solution.py:432
  206.5 13.9 %collective-permute-start.28 = (bf16[1024,256]{1,0:T(8,128)(2,1)}, bf16[1024,256]{1,0:T(8,128)(2,1)}, u32[]{:S(2)}, u32[]{:S(2)}) collective-permute-start(bf16[1024,256]{1,0:T(8,128)(2,1)} %get-tuple-element.83.refs_13_), channel_id=1, source_target_pairs={{8,0},{16,8},{24,16},{28,24},{20,28},{12,20},{4,12},{0,4},{9,1},{1... | collective-permute-start | bytes 1572872 | tf_op jit(solution)/shard_map/ppermute | solution.py:432
  208.5 15.4 %collective-permute-start.33 = (bf16[1024,256]{1,0:T(8,128)(2,1)}, bf16[1024,256]{1,0:T(8,128)(2,1)}, u32[]{:S(2)}, u32[]{:S(2)}) collective-permute-start(bf16[1024,256]{1,0:T(8,128)(2,1)} %add_convert_fusion.2.refs_2_), channel_id=1, source_target_pairs={{0,2},{1,3},{2,0},{3,1},{4,6},{5,7},{6,4},{7,5},{8,10},{9,11},{10,... | collective-permute-start | bytes 1572872 | tf_op jit(solution)/shard_map/ppermute | solution.py:431
  251.6 15.2 %collective-permute-start.37 = (bf16[1024,256]{1,0:T(8,128)(2,1)}, bf16[1024,256]{1,0:T(8,128)(2,1)}, u32[]{:S(2)}, u32[]{:S(2)}) collective-permute-start(bf16[1024,256]{1,0:T(8,128)(2,1)} %get-tuple-element.99), channel_id=1, source_target_pairs={{0,1},{1,0},{2,3},{3,2},{4,5},{5,4},{6,7},{7,6},{8,9},{9,8},{10,11... | collective-permute-start | bytes 1572872 | tf_op jit(solution)/shard_map/ppermute | solution.py:431
  258.0 13.2 %collective-permute-start.39 = (bf16[1024,256]{1,0:T(8,128)(2,1)}, bf16[1024,256]{1,0:T(8,128)(2,1)S(1)}, u32[]{:S(2)}, u32[]{:S(2)}) collective-permute-start(bf16[1024,256]{1,0:T(8,128)(2,1)} %add_convert_fusion), channel_id=1, source_target_pairs={{0,2},{1,3},{2,0},{3,1},{4,6},{5,7},{6,4},{7,5},{8,10},{9,11},{10,... | collective-permute-start | bytes 1572872 | tf_op jit(solution)/shard_map/ppermute | solution.py:431
  (51 other events, 326.2 us)
